TPU v7x, 32 devices: a whole 2x2x4 slice. The times are simulated.
32 devices in a mesh: dp: 8 (over z, x), tensor: 4 (over y, core).
Axes of the slice: x: 2, y: 2, z: 4, core: 2. Of those that a mesh axis runs over, the one named last changes fastest.
Arguments:
- tokens: bfloat16 [32, 1024, 512], P(('dp', 'tensor')), may hold values from -6 to 6
- clip_ids: int32 [32, 1024], P('dp'), may hold values from 0 to 15, never falling along the last dimension, each value on 1 to 128 neighbouring positions
- ln1_gain: float32 [512], replicated, may hold values from 0.5 to 1.5
- ln1_bias: float32 [512], replicated, may hold values from -3 to 3
- query_key_value_weight: bfloat16 [512, 3, 512], P(None, None, 'tensor'), may hold values from -0.25 to 0.25
- projection_weight: bfloat16 [512, 512], P('tensor'), may hold values from -0.75 to 0.75
- attention_output_bias: float32 [512], replicated, may hold values from -3 to 3
- ln2_gain: float32 [512], replicated, may hold values from 0.5 to 1.5
- ln2_bias: float32 [512], replicated, may hold values from -3 to 3
- up_weight: bfloat16 [512, 2048], P(None, 'tensor'), may hold values from -0.25 to 0.25
- mlp_up_bias: float32 [2048], P('tensor'), may hold values from -3 to 3
- down_weight: bfloat16 [2048, 512], P('tensor'), may hold values from -0.1875 to 0.1875
- mlp_down_bias: float32 [512], replicated, may hold values from -3 to 3
- grad_output: bfloat16 [32, 1024, 512], P(('dp', 'tensor')), may hold values from -6 to 6
Outputs:
- output: bfloat16 [32, 1024, 512], P(('dp', 'tensor'))
- grad_tokens: bfloat16 [32, 1024, 512], P(('dp', 'tensor'))
- g_ln1_gain: float32 [512], P(('dp', 'tensor'))
- g_ln1_bias: float32 [512], P(('dp', 'tensor'))
- query_key_value_gradient: float32 [512, 3, 512], P('dp', None, 'tensor')
- projection_weight_gradient: float32 [512, 512], P('tensor', 'dp')
- g_proj_bias: float32 [512], P(('dp', 'tensor'))
- g_ln2_gain: float32 [512], P(('dp', 'tensor'))
- g_ln2_bias: float32 [512], P(('dp', 'tensor'))
- up_weight_gradient: float32 [512, 2048], P('dp', 'tensor')
- g_up_bias: float32 [4, 512], P('tensor', 'dp')
- down_weight_gradient: float32 [2048, 512], P('tensor', 'dp')
- g_down_bias: float32 [512], P(('dp', 'tensor'))
Inputs may be any that keep to these rules, and one draw needn't show every extreme that they name: `clip_ids`: within a sequence clip numbers never fall from one time step to the next; each clip holds 1 to 128 time steps, and some clip exactly 128.
All inputs are finite; a program needn't handle non-finite values.
Results may differ from a plain program's by a relative error of at most 0.019.
Values may be sent and summed in bfloat16 or wider, within the bound.
A program may use at most 192 MiB of HBM per device.

v0:
```python
import jax
import jax.numpy as jnp
from jax import lax
from jax.sharding import PartitionSpec as P

HD = 64


epsilon = 1e-05


def layer_norm(values, gain, shift):
    centre = values - jnp.mean(values, axis=-1, keepdims=True)
    spread = jnp.mean(centre * centre, axis=-1, keepdims=True)
    return centre * lax.rsqrt(spread + epsilon) * gain + shift


def gelu_exact(values):
    return jax.nn.gelu(values, approximate=False)


def visible(clip_row, start, count):
    length = clip_row.shape[0]
    query_pos = start + jnp.arange(count)
    key_pos = jnp.arange(length)
    query_clip = clip_row[start : start + count]
    return (key_pos[None, :] <= query_pos[:, None]) & (query_clip[:, None] == clip_row[None, :])


def block_scores(query, keys, clip_row, start, block):
    scale = query.shape[-1] ** (-0.5)
    allowed = visible(clip_row, start, block)
    scores = (
        jnp.einsum(
            "qhd,khd->hqk", query[start : start + block], keys, preferred_element_type=jnp.float32
        )
        * scale
    )
    return (jnp.where(allowed[None], scores, -1e30), allowed)


def attend_sequence(pieces):
    query, keys, vals, clip_row = pieces
    length = query.shape[0]
    block = min(512, length)
    outs = []
    sums = []
    for start in range(0, length, block):
        scores, allowed = block_scores(query, keys, clip_row, start, block)
        peak = jnp.max(scores, axis=-1, keepdims=True)
        expo = jnp.exp(scores - peak)
        total = jnp.sum(expo, axis=-1, keepdims=True)
        probs = (expo / total).astype(jnp.bfloat16)
        outs.append(jnp.einsum("hqk,khd->qhd", probs, vals, preferred_element_type=jnp.float32))
        sums.append((peak + jnp.log(total))[..., 0])
    return (jnp.concatenate(outs, 0), jnp.concatenate(sums, 1))


def attend_back(pieces):
    query, keys, vals, clip_row, lse, grad_mixed = pieces
    length = query.shape[0]
    block = min(512, length)
    scale = query.shape[-1] ** (-0.5)
    grad_keys = jnp.zeros(keys.shape, jnp.float32)
    grad_vals = jnp.zeros(vals.shape, jnp.float32)
    query_parts = []
    for start in range(0, length, block):
        scores, allowed = block_scores(query, keys, clip_row, start, block)
        probs_f = jnp.where(
            allowed[None], jnp.exp(scores - lse[:, start : start + block, None]), 0.0
        )
        probs = probs_f.astype(jnp.bfloat16)
        grad_block = grad_mixed[start : start + block]
        dprobs = jnp.einsum("qhd,khd->hqk", grad_block, vals, preferred_element_type=jnp.float32)
        grad_vals = grad_vals + jnp.einsum(
            "hqk,qhd->khd", probs, grad_block, preferred_element_type=jnp.float32
        )
        inner = jnp.sum(probs_f * dprobs, axis=-1, keepdims=True)
        dscores = (probs_f * (dprobs - inner)).astype(jnp.bfloat16)
        query_parts.append(
            jnp.einsum("hqk,khd->qhd", dscores, keys, preferred_element_type=jnp.float32) * scale
        )
        grad_keys = (
            grad_keys
            + jnp.einsum(
                "hqk,qhd->khd",
                dscores,
                query[start : start + block],
                preferred_element_type=jnp.float32,
            )
            * scale
        )
    return (jnp.concatenate(query_parts, 0), grad_keys, grad_vals)


def on_device(
    tokens,
    clip_ids,
    ln1_gain,
    ln1_bias,
    query_key_value_weight,
    projection_weight,
    attention_output_bias,
    ln2_gain,
    ln2_bias,
    up_weight,
    mlp_up_bias,
    down_weight,
    mlp_down_bias,
    grad_output,
):
    head_size = HD
    local_width = query_key_value_weight.shape[2]
    local_heads = local_width // head_size
    tok_f = tokens.astype(jnp.float32)
    first_normalized = layer_norm(tok_f, ln1_gain, ln1_bias).astype(jnp.bfloat16)
    first_normalized_every = lax.all_gather(first_normalized, "tensor", axis=0, tiled=True)
    seqs = first_normalized_every.shape[0]
    length = first_normalized_every.shape[1]
    query_key_value_rows = jnp.einsum(
        "tre,eub->trub",
        first_normalized_every,
        query_key_value_weight,
        preferred_element_type=jnp.float32,
    ).astype(jnp.bfloat16)
    query_key_value_rows = query_key_value_rows.reshape(seqs, length, 3, local_heads, head_size)
    query = query_key_value_rows[:, :, 0]
    keys = query_key_value_rows[:, :, 1]
    vals = query_key_value_rows[:, :, 2]
    mixed_heads_output, lse = lax.map(attend_sequence, (query, keys, vals, clip_ids))
    mixed_heads_lowered = mixed_heads_output.astype(jnp.bfloat16).reshape(seqs, length, local_width)
    attention_piece = jnp.einsum(
        "bne,eo->bno", mixed_heads_lowered, projection_weight, preferred_element_type=jnp.float32
    )
    attn_rows = lax.psum_scatter(
        attention_piece.astype(jnp.bfloat16), "tensor", scatter_dimension=0, tiled=True
    ).astype(jnp.float32)
    hidden_activation = tok_f + attn_rows + attention_output_bias
    second_normalized = layer_norm(hidden_activation, ln2_gain, ln2_bias).astype(jnp.bfloat16)
    second_normalized_every = lax.all_gather(second_normalized, "tensor", axis=0, tiled=True)
    upper_half_rows = (
        jnp.einsum(
            "wih,hm->wim", second_normalized_every, up_weight, preferred_element_type=jnp.float32
        )
        + mlp_up_bias
    )
    active_rows_now = gelu_exact(upper_half_rows).astype(jnp.bfloat16)
    perceptron_piece = jnp.einsum(
        "bne,eo->bno", active_rows_now, down_weight, preferred_element_type=jnp.float32
    )
    mlp_rows = lax.psum_scatter(
        perceptron_piece.astype(jnp.bfloat16), "tensor", scatter_dimension=0, tiled=True
    ).astype(jnp.float32)
    output = (hidden_activation + mlp_rows + mlp_down_bias).astype(jnp.bfloat16)
    gradient_every_row = lax.all_gather(grad_output, "tensor", axis=0, tiled=True)
    down_weight_gradient = jnp.einsum(
        "egz,egb->zb", active_rows_now, gradient_every_row, preferred_element_type=jnp.float32
    )
    gradient_active_rows = jnp.einsum(
        "etk,ok->eto", gradient_every_row, down_weight, preferred_element_type=jnp.float32
    )
    gradient_upper_half = jax.vjp(gelu_exact, upper_half_rows)[1](gradient_active_rows)[0].astype(
        jnp.bfloat16
    )
    g_up_bias = jnp.sum(gradient_upper_half, axis=(0, 1), dtype=jnp.float32)
    up_weight_gradient = jnp.einsum(
        "kjy,kjt->yt",
        second_normalized_every,
        gradient_upper_half,
        preferred_element_type=jnp.float32,
    )
    grad_normed2_part = jnp.einsum(
        "hwm,bm->hwb", gradient_upper_half, up_weight, preferred_element_type=jnp.float32
    )
    grad_normed2 = lax.psum_scatter(
        grad_normed2_part.astype(jnp.bfloat16), "tensor", scatter_dimension=0, tiled=True
    ).astype(jnp.float32)
    grad_hidden_ln, g_ln2_gain, g_ln2_bias = jax.vjp(
        layer_norm, hidden_activation, ln2_gain, ln2_bias
    )[1](grad_normed2)
    grad_f = grad_output.astype(jnp.float32)
    grad_hidden = grad_f + grad_hidden_ln
    g_down_bias = jnp.sum(grad_f, axis=(0, 1))
    g_proj_bias = jnp.sum(grad_hidden, axis=(0, 1))
    branch_low = grad_hidden.astype(jnp.bfloat16)
    branch_every_row = lax.all_gather(branch_low, "tensor", axis=0, tiled=True)
    projection_weight_gradient = jnp.einsum(
        "egz,egb->zb", mixed_heads_lowered, branch_every_row, preferred_element_type=jnp.float32
    )
    grad_mixed = jnp.einsum(
        "etk,ok->eto", branch_every_row, projection_weight, preferred_element_type=jnp.float32
    ).astype(jnp.bfloat16)
    grad_mixed = grad_mixed.reshape(seqs, length, local_heads, head_size)
    grad_query, grad_keys, grad_vals = lax.map(
        attend_back, (query, keys, vals, clip_ids, lse, grad_mixed)
    )
    gradient_query_key_value = (
        jnp.stack((grad_query, grad_keys, grad_vals), axis=2)
        .astype(jnp.bfloat16)
        .reshape(seqs, length, 3, local_width)
    )
    query_key_value_gradient = jnp.einsum(
        "zny,znqj->yqj",
        first_normalized_every,
        gradient_query_key_value,
        preferred_element_type=jnp.float32,
    )
    grad_normed_part = jnp.einsum(
        "kegu,hgu->keh",
        gradient_query_key_value,
        query_key_value_weight,
        preferred_element_type=jnp.float32,
    )
    grad_normed = lax.psum_scatter(
        grad_normed_part.astype(jnp.bfloat16), "tensor", scatter_dimension=0, tiled=True
    ).astype(jnp.float32)
    grad_tok_ln, g_ln1_gain, g_ln1_bias = jax.vjp(layer_norm, tok_f, ln1_gain, ln1_bias)[1](
        grad_normed
    )
    grad_tokens = (grad_hidden + grad_tok_ln).astype(jnp.bfloat16)
    g_qkv_s, g_proj_s, g_up_s, g_up_bias_s, g_down_s = (
        lax.psum_scatter(
            query_key_value_gradient.astype(jnp.bfloat16), "dp", scatter_dimension=0, tiled=True
        ).astype(jnp.float32),
        lax.psum_scatter(
            projection_weight_gradient.astype(jnp.bfloat16), "dp", scatter_dimension=1, tiled=True
        ).astype(jnp.float32),
        lax.psum_scatter(
            up_weight_gradient.astype(jnp.bfloat16), "dp", scatter_dimension=0, tiled=True
        ).astype(jnp.float32),
        lax.psum_scatter(
            g_up_bias[None].astype(jnp.bfloat16), "dp", scatter_dimension=1, tiled=True
        ).astype(jnp.float32),
        lax.psum_scatter(
            down_weight_gradient.astype(jnp.bfloat16), "dp", scatter_dimension=1, tiled=True
        ).astype(jnp.float32),
    )
    v_ln1_gain, v_ln1_bias, v_proj_bias, v_ln2_gain, v_ln2_bias, v_down_bias = (
        lax.psum_scatter(g_ln1_gain, ("dp", "tensor"), scatter_dimension=0, tiled=True),
        lax.psum_scatter(g_ln1_bias, ("dp", "tensor"), scatter_dimension=0, tiled=True),
        lax.psum_scatter(g_proj_bias, ("dp", "tensor"), scatter_dimension=0, tiled=True),
        lax.psum_scatter(g_ln2_gain, ("dp", "tensor"), scatter_dimension=0, tiled=True),
        lax.psum_scatter(g_ln2_bias, ("dp", "tensor"), scatter_dimension=0, tiled=True),
        lax.psum_scatter(g_down_bias, ("dp", "tensor"), scatter_dimension=0, tiled=True),
    )
    return (
        output,
        grad_tokens,
        v_ln1_gain,
        v_ln1_bias,
        g_qkv_s,
        g_proj_s,
        v_proj_bias,
        v_ln2_gain,
        v_ln2_bias,
        g_up_s,
        g_up_bias_s,
        g_down_s,
        v_down_bias,
    )


def solution(mesh):
    in_specs = (
        P(("dp", "tensor"), None, None),
        P("dp", None),
        P(),
        P(),
        P(None, None, "tensor"),
        P("tensor", None),
        P(),
        P(),
        P(),
        P(None, "tensor"),
        P("tensor"),
        P("tensor", None),
        P(),
        P(("dp", "tensor"), None, None),
    )
    out_specs = (
        P(("dp", "tensor"), None, None),
        P(("dp", "tensor"), None, None),
        P(("dp", "tensor")),
        P(("dp", "tensor")),
        P("dp", None, "tensor"),
        P("tensor", "dp"),
        P(("dp", "tensor")),
        P(("dp", "tensor")),
        P(("dp", "tensor")),
        P("dp", "tensor"),
        P("tensor", "dp"),
        P("tensor", "dp"),
        P(("dp", "tensor")),
    )
    return jax.shard_map(
        on_device, mesh=mesh, in_specs=in_specs, out_specs=out_specs, check_vma=False
    )
```

profile of v0, /device:TPU:0, one launch (start us, length us, event | category | flops | bytes accessed | tf_op | source)
XLA Modules:
  0.0 804.0 jit_solution(4226196650946657626)
XLA Ops:
  10.5 2.7 fusion.98
  13.3 37.3 %all-gather.5.cloned.1.call-done = bf16[4,1024,512]{2,1,0:T(8,128)(2,1)} async-done(((bf16[1,1024,512]{2,1,0:T(8,128)(2,1)}), bf16[4,1024,512]{2,1,0:T(8,128)(2,1)}) %all-gather.5.cloned.1.call-update) | async-done | bytes 4194320 | tf_op jit(solution)/shard_map/all_gather | solution.py:117
  50.6 4.0 fusion.94
  57.4 46.1 %while.26 = (s32[]{:T(128)}, bf16[4,1024,2,64]{1,3,2,0:T(8,128)(2,1)}, f32[4,2,1024]{2,1,0:T(2,128)S(1)}, bf16[4,1024,2,64]{1,3,2,0:T(8,128)(2,1)}, s32[4,1024]{...) while((s32[]{:T(128)}, ...), condition=%wide.region_7.8_spmd, body=%wide.region_2.7_spmd.sunk | while | flops 565707264 | bytes 35764912 | solution.py:130
  62.6 2.4 fusion.189
  74.1 2.4 fusion.189
  85.6 2.4 fusion.189
  97.2 2.4 fusion.189
  103.5 4.8 convolution_convert_fusion.2
  108.4 44.6 %reduce-scatter.12.cloned.1.call-done = bf16[1,1024,512]{2,1,0:T(8,128)(2,1)} async-done(((bf16[4,1024,512]{2,1,0:T(8,128)(2,1)}), bf16[1,1024,512]{2,1,0:T(8,128)(2,1)}) %reduce-scatter.12.cloned.1.call-update) | async-done | bytes 1048592 | tf_op jit(solution)/shard_map/reduce_scatter | solution.py:135
  159.1 33.7 %all-gather.7.cloned.1.call-done = bf16[4,1024,512]{2,1,0:T(8,128)(2,1)} async-done(((bf16[1,1024,512]{2,1,0:T(8,128)(2,1)}), bf16[4,1024,512]{2,1,0:T(8,128)(2,1)}) %all-gather.7.cloned.1.call-update) | async-done | bytes 4194320 | tf_op jit(solution)/shard_map/all_gather | solution.py:140
  192.8 7.1 fusion.106
  199.9 4.0 copy-done.10
  203.9 20.4 %multiply_convert_fusion.2 = (bf16[4,1024,512]{2,1,0:T(8,128)(2,1)}, f32[4,1024,512]{2,1,0:T(8,128)}) fusion(f32[4,1024,512]{2,1,0:T(8,128)S(1)} %get-tuple-element.189, f32[512]{0:T(512)S(1)} %copy-done.28, u8[1024,512]{1,0:T(8,128)(4,1)S(1)} %get-tuple-element.111, u8[1024,512]{1,0:T(8,128)(4,1)S(1)} %get-tuple-element.110), kind=kLoop, calls=%fused_computation.116 | loop fusion | flops 148897792 | bytes 22022144 | tf_op jit(solution)/shard_map/convert_element_type | solution.py:147
  224.3 4.5 all-gather.9.cloned.1.call-done
  228.8 9.4 %fusion.136 = (bf16[512]{0:T(512)(128)(2,1)S(1)}, bf16[4,1024,512]{2,1,0:T(8,128)(2,1)S(1)}) fusion(f32[4,1024,512]{2,1,0:T(8,128)} %get-tuple-element.163, bf16[4,1024,512]{2,1,0:T(8,128)(2,1)} %all-gather.9.cloned.1.call-done, bf16[512,512]{1,0:T(8,128)(2,1)S(1)} %copy-done.31, f32[4,1024,512]{2,1,0:T(8,128)} %copy-done.10, f32[512]{0:T(512)S(1)} %copy-done.28), kind=kOutput, calls=%fused_computation.213 | convolution fusion | flops 2181037568 | bytes 25693184 | tf_op jit(solution)/shard_map/etk,ok->eto/dot_general | solution.py:159
  240.2 4.3 convolution_convert_fusion
  244.6 6.6 convolution_convert_fusion.1
  251.2 13.0 %all-gather.11.cloned.1.call-start = ((), (), s32[]{:S(2)}) async-start(), calls=%async_computation.15 | async-start | bytes 5242880 | tf_op jit(solution)/shard_map/all_gather | solution.py:186
  264.2 25.0 %reduce-scatter.16.cloned.1.call-done = bf16[1,1024,512]{2,1,0:T(8,128)(2,1)} async-done(((bf16[4,1024,512]{2,1,0:T(8,128)(2,1)}), bf16[1,1024,512]{2,1,0:T(8,128)(2,1)}) %reduce-scatter.16.cloned.1.call-update) | async-done | bytes 1048592 | tf_op jit(solution)/shard_map/reduce_scatter | solution.py:175
  289.2 2.2 convert_reduce_fusion.1
  291.4 2.6 fusion.103
  294.1 42.1 %reduce-scatter.14.cloned.1.call-done = bf16[1,1024,512]{2,1,0:T(8,128)(2,1)} async-done(((bf16[4,1024,512]{2,1,0:T(8,128)(2,1)}), bf16[1,1024,512]{2,1,0:T(8,128)(2,1)}) %reduce-scatter.14.cloned.1.call-update) | async-done | bytes 1048592 | tf_op jit(solution)/shard_map/reduce_scatter | solution.py:151
  336.2 3.7 fusion.133
  343.3 6.6 fusion.111
  350.1 7.4 fusion.110
  357.5 19.6 %all-gather.11.cloned.1.call-done = bf16[4,1024,512]{2,1,0:T(8,128)(2,1)} async-done(((bf16[1,1024,512]{2,1,0:T(8,128)(2,1)}), bf16[4,1024,512]{2,1,0:T(8,128)(2,1)}) %all-gather.11.cloned.1.call-update) | async-done | bytes 4194320 | tf_op jit(solution)/shard_map/all_gather | solution.py:186
  377.1 3.7 convolution_convert_fusion.3
  384.1 60.2 %while.27 = (s32[]{:T(128)}, bf16[4,1024,2,64]{1,3,2,0:T(8,128)(2,1)}, bf16[4,1024,2,64]{1,3,2,0:T(8,128)(2,1)}, bf16[4,1024,2,64]{1,3,2,0:T(8,128)(2,1)}, bf16[...) while((s32[]{:T(128)}, ...), condition=%wide.region_18.19_spmd, body=%wide.region_15.18_spmd.sunk | while | flops 1367472640 | bytes 96825176 | solution.py:194
  387.1 2.1 multiply_reduce_fusion.5
  402.1 2.1 multiply_reduce_fusion.5
  417.2 2.1 multiply_reduce_fusion.5
  432.2 2.1 multiply_reduce_fusion.5
  444.3 2.4 copy.62
  446.7 2.3 copy.60
  448.9 2.3 copy.61
  451.2 4.6 fusion.118
  456.2 6.4 fusion.115
  462.6 5.9 bitcast_convert_fusion
  469.9 37.2 %reduce-scatter.26.cloned.1.call-done = bf16[512,64]{0,1:T(8,128)(2,1)} async-done(((bf16[512,512]{0,1:T(8,128)(2,1)}), bf16[512,64]{0,1:T(8,128)(2,1)}) %reduce-scatter.26.cloned.1.call-update) | async-done | bytes 65552 | tf_op jit(solution)/shard_map/reduce_scatter | solution.py:234
  508.6 62.6 %reduce-scatter.24.cloned.1.call-done = bf16[64,512]{1,0:T(8,128)(2,1)} async-done(((bf16[512,512]{1,0:T(8,128)(2,1)}), bf16[64,512]{1,0:T(8,128)(2,1)}) %reduce-scatter.24.cloned.1.call-update) | async-done | bytes 65552 | tf_op jit(solution)/shard_map/reduce_scatter | solution.py:228
  572.8 62.1 %reduce-scatter.22.cloned.1.call-done = bf16[128,64]{0,1:T(8,128)(2,1)} async-done(((bf16[128,512]{0,1:T(8,128)(2,1)}), bf16[128,64]{0,1:T(8,128)(2,1)}) %reduce-scatter.22.cloned.1.call-update) | async-done | bytes 16400 | tf_op jit(solution)/shard_map/reduce_scatter | solution.py:225
  636.2 63.9 %reduce-scatter.20.cloned.1.call-done = bf16[64,3,128]{2,0,1:T(8,128)(2,1)} async-done(((bf16[512,3,128]{2,0,1:T(8,128)(2,1)}), bf16[64,3,128]{2,0,1:T(8,128)(2,1)}) %reduce-scatter.20.cloned.1.call-update) | async-done | bytes 49168 | tf_op jit(solution)/shard_map/reduce_scatter | solution.py:222
  701.6 44.8 %reduce-scatter.18.cloned.1.call-done = bf16[1,1024,512]{2,1,0:T(8,128)(2,1)} async-done(((bf16[4,1024,512]{2,1,0:T(8,128)(2,1)}), bf16[1,1024,512]{2,1,0:T(8,128)(2,1)}) %reduce-scatter.18.cloned.1.call-update) | async-done | bytes 1048592 | tf_op jit(solution)/shard_map/reduce_scatter | solution.py:214
  746.4 2.2 convert_reduce_fusion
  748.6 2.4 fusion.104
  751.0 39.5 %all-reduce.6 = (f32[512]{0:T(512)S(1)}, f32[512]{0:T(512)S(1)}, f32[512]{0:T(512)S(1)}, f32[512]{0:T(512)S(1)}, f32[512]{0:T(512)S(1)}, /*index=5*/f32[512]{0:T(512)S(1)}) all-reduce(f32[512]{0:T(512)S(1)} %get-tuple-element.114, f32[512]{0:T(512)S(1)} %get-tuple-element.118, ...), channel_id=6, replica_groups=mesh['dp'=8,'tensor'=4] {'dp','tensor'}, use_global_device_ids=true, to_apply=%region_23.24.clone | all-reduce | flops 3072 | bytes 24576
  794.1 3.0 add_convert_fusion.1
  (290 shorter events, 119.8 us)
Async XLA Ops:
  7.2 185.6 %copy-start = (bf16[512,512]{1,0:T(8,128)(2,1)S(1)}, bf16[512,512]{1,0:T(8,128)(2,1)}, u32[]{:S(2)}) copy-start(bf16[512,512]{1,0:T(8,128)(2,1)} %param.27) | copy-start | bytes 1572868
  7.2 43.4 %copy-start.32 = (bf16[512,3,128]{2,0,1:T(8,128)(2,1)S(1)}, bf16[512,3,128]{2,0,1:T(8,128)(2,1)}, u32[]{:S(2)}) copy-start(bf16[512,3,128]{2,0,1:T(8,128)(2,1)} %param.22) | copy-start | bytes 1179652
  7.2 43.3 %all-gather.5.cloned.1.call-start = ((), (), s32[]{:S(2)}) async-start(), calls=%async_computation.9 | async-start | bytes 5242880 | tf_op jit(solution)/shard_map/all_gather | solution.py:117
  8.8 45.8 %copy-start.19 = (f32[1024]{0:T(1024)}, f32[1024]{0:T(1024)S(1)}, u32[]{:S(2)}) copy-start(f32[1024]{0:T(1024)S(1)} %broadcast_multiply_fusion.1) | copy-start | bytes 12292
  10.5 44.1 %copy-start.24 = (f32[1024]{0:T(1024)}, f32[1024]{0:T(1024)S(1)}, u32[]{:S(2)}) copy-start(f32[1024]{0:T(1024)S(1)} %fusion.100) | copy-start | bytes 12292
  10.5 44.1 %copy-start.22 = (f32[1024]{0:T(1024)}, f32[1024]{0:T(1024)S(1)}, u32[]{:S(2)}) copy-start(f32[1024]{0:T(1024)S(1)} %fusion.128) | copy-start | bytes 12292
  13.2 139.8 %reduce-scatter.12.cloned.1.call-start = ((), (), s32[]{:S(2)}) async-start(), calls=%async_computation.10 | async-start | bytes 5242880 | tf_op jit(solution)/shard_map/reduce_scatter | solution.py:135
  54.6 2.7 copy-start.18
  57.4 46.1 %copy-start.17 = (bf16[128,512]{1,0:T(8,128)(2,1)S(1)}, bf16[128,512]{1,0:T(8,128)(2,1)}, u32[]{:S(2)}) copy-start(bf16[128,512]{1,0:T(8,128)(2,1)} %param.23) | copy-start | bytes 393220
  62.6 2.4 copy-start.7
  103.4 4.9 copy-start.5
  103.5 49.5 %copy-start.2 = (bf16[1,1024,512]{2,1,0:T(8,128)(2,1)S(1)}, bf16[1,1024,512]{2,1,0:T(8,128)(2,1)}, u32[]{:S(2)}) copy-start(bf16[1,1024,512]{2,1,0:T(8,128)(2,1)} %param.18) | copy-start | bytes 3145732
  103.5 49.5 %copy-start.21 = (f32[512]{0:T(512)S(1)}, f32[512]{0:T(512)}, u32[]{:S(2)}) copy-start(f32[512]{0:T(512)} %param.24) | copy-start | bytes 6148
  108.3 48.3 %copy-start.27 = (f32[512]{0:T(512)S(1)}, f32[512]{0:T(512)}, u32[]{:S(2)}) copy-start(f32[512]{0:T(512)} %param.25) | copy-start | bytes 6148
  108.3 48.3 %copy-start.29 = (f32[512]{0:T(512)S(1)}, f32[512]{0:T(512)}, u32[]{:S(2)}) copy-start(f32[512]{0:T(512)} %param.26) | copy-start | bytes 6148
  108.3 84.5 %all-gather.7.cloned.1.call-start = ((), (), s32[]{:S(2)}) async-start(), calls=%async_computation.11 | async-start | bytes 5242880 | tf_op jit(solution)/shard_map/all_gather | solution.py:140
  153.0 3.6 copy-start.3
  154.7 38.1 %copy-start.28 = (f32[512]{0:T(512)S(1)}, f32[512]{0:T(512)}, u32[]{:S(2)}) copy-start(f32[512]{0:T(512)} %param.28) | copy-start | bytes 6148
  158.2 70.6 %all-gather.9.cloned.1.call-start = ((), (), s32[]{:S(2)}) async-start(), calls=%async_computation.13 | async-start | bytes 5242880 | tf_op jit(solution)/shard_map/all_gather | solution.py:155
  158.8 130.4 %reduce-scatter.16.cloned.1.call-start = ((), (), s32[]{:S(2)}) async-start(), calls=%async_computation.14 | async-start | bytes 5242880 | tf_op jit(solution)/shard_map/reduce_scatter | solution.py:175
  199.9 4.0 copy-start.10
  203.9 24.9 %copy-start.31 = (bf16[512,512]{1,0:T(8,128)(2,1)S(1)}, bf16[512,512]{1,0:T(8,128)(2,1)}, u32[]{:S(2)}) copy-start(bf16[512,512]{1,0:T(8,128)(2,1)} %param.29) | copy-start | bytes 1572868
  244.5 91.6 %reduce-scatter.14.cloned.1.call-start = ((), (), s32[]{:S(2)}) async-start(), calls=%async_computation.12 | async-start | bytes 5242880 | tf_op jit(solution)/shard_map/reduce_scatter | solution.py:151
  251.2 85.0 %copy-start.30 = (f32[512]{0:T(512)S(1)}, f32[512]{0:T(512)}, u32[]{:S(2)}) copy-start(f32[512]{0:T(512)} %param.30) | copy-start | bytes 6148
  251.2 125.9 %all-gather.11.cloned.1.call-start = ((), (), s32[]{:S(2)}) async-start(), calls=%async_computation.15 | async-start | bytes 5242880 | tf_op jit(solution)/shard_map/all_gather | solution.py:186
  342.4 126.2 %reduce-scatter.28.cloned.1.call-start = ((), (), s32[]{:S(2)}) async-start(), calls=%async_computation.21 | async-start | bytes 147456
  343.3 163.8 %reduce-scatter.26.cloned.1.call-start = ((), (), s32[]{:S(2)}) async-start(), calls=%async_computation.20 | async-start | bytes 589824 | tf_op jit(solution)/shard_map/reduce_scatter | solution.py:234
  350.0 221.2 %reduce-scatter.24.cloned.1.call-start = ((), (), s32[]{:S(2)}) async-start(), calls=%async_computation.19 | async-start | bytes 589824 | tf_op jit(solution)/shard_map/reduce_scatter | solution.py:228
  357.4 277.4 %reduce-scatter.22.cloned.1.call-start = ((), (), s32[]{:S(2)}) async-start(), calls=%async_computation.18 | async-start | bytes 147456 | tf_op jit(solution)/shard_map/reduce_scatter | solution.py:225
  384.1 2.9 copy-start.6
  384.1 3.0 copy-start.11
  399.2 2.9 copy-start.6
  399.2 3.0 copy-start.11
  414.2 2.9 copy-start.6
  414.2 3.0 copy-start.11
  429.3 2.9 copy-start.6
  429.3 3.0 copy-start.11
  444.3 6.9 copy-start.9
  455.9 6.7 copy-start.16
  455.9 6.7 copy-start.33
  455.9 244.2 %reduce-scatter.20.cloned.1.call-start = ((), (), s32[]{:S(2)}) async-start(), calls=%async_computation.17 | async-start | bytes 442368 | tf_op jit(solution)/shard_map/reduce_scatter | solution.py:222
  462.6 283.8 %reduce-scatter.18.cloned.1.call-start = ((), (), s32[]{:S(2)}) async-start(), calls=%async_computation.16 | async-start | bytes 5242880 | tf_op jit(solution)/shard_map/reduce_scatter | solution.py:214
  468.5 277.8 %copy-start.20 = (f32[1024]{0:T(1024)S(1)}, f32[1024]{0:T(1024)}, u32[]{:S(2)}) copy-start(f32[1024]{0:T(1024)} %copy-done.19) | copy-start | bytes 12292
  468.5 277.8 %copy-start.26 = (f32[512]{0:T(512)S(1)}, f32[512]{0:T(512)}, u32[]{:S(2)}) copy-start(f32[512]{0:T(512)} %param.20) | copy-start | bytes 6148
  468.5 280.0 %copy-start.25 = (f32[1024]{0:T(1024)S(1)}, f32[1024]{0:T(1024)}, u32[]{:S(2)}) copy-start(f32[1024]{0:T(1024)} %copy-done.24) | copy-start | bytes 12292
  468.5 280.1 %copy-start.23 = (f32[1024]{0:T(1024)S(1)}, f32[1024]{0:T(1024)}, u32[]{:S(2)}) copy-start(f32[1024]{0:T(1024)} %copy-done.22) | copy-start | bytes 12292
  746.4 47.7 %copy-start.8 = (bf16[1,1024,512]{2,1,0:T(8,128)(2,1)S(1)}, bf16[1,1024,512]{2,1,0:T(8,128)(2,1)}, u32[]{:S(2)}) copy-start(bf16[1,1024,512]{2,1,0:T(8,128)(2,1)} %reduce-scatter.18.cloned.1.call-done) | copy-start | bytes 3145732
  746.4 50.7 %copy-start.1 = (bf16[512,512]{1,0:T(8,128)(2,1)S(1)}, bf16[512,512]{1,0:T(8,128)(2,1)}, u32[]{:S(2)}) copy-start(bf16[512,512]{1,0:T(8,128)(2,1)} %param.27) | copy-start | bytes 1572868
  (21 other events, 34.0 us)
Sparse Core Ops, SparseCore 0:
  13.3 37.1 all-gather.4
  108.4 44.4 reduce-scatter.11
  158.3 34.4 all-gather.6
  194.3 34.4 all-gather.8
  244.6 44.5 reduce-scatter.15
  291.6 44.5 reduce-scatter.13
  342.5 34.4 all-gather.10
  381.3 61.0 reduce-scatter.27
  446.1 60.9 reduce-scatter.25
  510.3 60.8 reduce-scatter.23
  574.9 59.8 reduce-scatter.21
  638.9 61.1 reduce-scatter.19
  702.8 43.4 reduce-scatter.17
where the time goes:
time: 814 us; the launch traced here: 804 us
  waiting for transfers between devices  478 us (59%)
  matrix products  143 us (18%)
  other arithmetic  83.4 us (10%)
  blocking collectives  39.5 us (5%)
  local copies, waits for them, and re-layouts  30.6 us (4%)
  between operations  14.7 us (2%)
  starting transfers between devices  14 us (2%)
    reduce_scatter x1, waiting for transfers between devices, on_device(): lax.psum_scatter(query_key_value_gradient.astype(jnp.bfloat16), 'dp', sca...  63.9 us
    reduce_scatter x1, waiting for transfers between devices, on_device(): lax.psum_scatter(up_weight_gradient.astype(jnp.bfloat16), 'dp', scatter_d...  62.6 us
    reduce_scatter x1, waiting for transfers between devices, on_device(): lax.psum_scatter(projection_weight_gradient.astype(jnp.bfloat16), 'dp', s...  62.1 us
    reduce_scatter x1, waiting for transfers between devices, on_device(): lax.psum_scatter(grad_normed_part.astype(jnp.bfloat16), 'tensor', scatter...  44.8 us
    reduce_scatter x1, waiting for transfers between devices, on_device(): lax.psum_scatter(attention_piece.astype(jnp.bfloat16), 'tensor', scatter_...  44.6 us
    reduce_scatter x1, waiting for transfers between devices, on_device(): lax.psum_scatter(perceptron_piece.astype(jnp.bfloat16), 'tensor', scatter...  42.1 us
    unnamed x1, blocking collectives  39.5 us
    all_gather x1, waiting for transfers between devices, on_device(): lax.all_gather(first_normalized, 'tensor', axis=0, tiled=True)  37.3 us
  transfers between devices with their start and end apart: 13, of which 12 were waited for; matrix products, arithmetic and copies ran while one was open for 18% of the time, Pallas kernels for 0%

commit v1 on v0

--- a/solution.py
+++ b/solution.py
@@ -1,9 +1,19 @@
+import functools
+import math
+
 import jax
 import jax.numpy as jnp
 from jax import lax
+from jax.experimental import pallas as pl
+from jax.experimental.pallas import tpu as pltpu
 from jax.sharding import PartitionSpec as P
 
 HD = 64
+CORES = 2
+WIDE = 2
+BF = jnp.bfloat16
+F32 = jnp.float32
+MESH = pl.DeviceIdType.MESH
 
 
 epsilon = 1e-05
@@ -260,6 +270,740 @@
     )
 
 
+BLOCK = 128
+ROWS = 256
+
+
+def mm(left, right):
+    return lax.dot_general(left, right, (((1,), (0,)), ((), ())), preferred_element_type=F32)
+
+
+def mm_nt(left, right):
+    return lax.dot_general(left, right, (((1,), (1,)), ((), ())), preferred_element_type=F32)
+
+
+def normal_parts(u):
+    bell = jnp.exp2(u * u * (-0.5 * math.log2(math.e)))
+    base = 1.0 + jnp.abs(u) * (0.3275911 * math.sqrt(0.5))
+    t = pl.reciprocal(base, approx=True)
+    t = t * (2.0 - base * t)
+    poly = 0.5 * 1.061405429
+    poly = poly * t - 0.5 * 1.453152027
+    poly = poly * t + 0.5 * 1.421413741
+    poly = poly * t - 0.5 * 0.284496736
+    poly = poly * t + 0.5 * 0.254829592
+    half = poly * t * bell
+    cdf = jnp.where(u >= 0.0, 1.0 - half, half)
+    return cdf, u * bell * (1.0 / math.sqrt(2.0 * math.pi))
+
+
+def by_eight(values):
+    return jnp.sum(values.reshape(-1, 8, values.shape[-1]), axis=0)
+
+
+class Copies:
+    def __init__(self, send, recv):
+        self.send, self.recv, self.made, self.started = send, recv, {}, []
+
+    def describe(self, name, src, dst, device):
+        at = self.made.setdefault(name, len(self.made))
+        return pltpu.make_async_remote_copy(
+            src_ref=src,
+            dst_ref=dst,
+            send_sem=self.send.at[at],
+            recv_sem=self.recv.at[at],
+            device_id=device,
+            device_id_type=MESH,
+        )
+
+    def start(self, name, src, dst, device):
+        copy = self.describe(name, src, dst, device)
+        copy.start()
+        self.started.append(copy)
+
+    def arrived(self, name, dst, device):
+        self.describe(name, dst, dst, device).wait_recv()
+
+    def drain(self):
+        for copy in self.started:
+            copy.wait_send()
+
+
+def layer_kernel(
+    sizes,
+    tok_h,
+    dy_h,
+    clip_ref,
+    vecs_ref,
+    bu_ref,
+    wq_h,
+    wp_h,
+    wu_h,
+    wd_h,
+    out_h,
+    gtok_h,
+    gm_ref,
+    gq_ref,
+    gv_ref,
+    tok,
+    dy,
+    dy_t,
+    wq,
+    wp,
+    wu,
+    wd,
+    bu,
+    n1,
+    n1_t,
+    stats,
+    qs,
+    ks,
+    vs,
+    ks_t,
+    vs_t,
+    bias,
+    probs,
+    mixed,
+    hidden,
+    n2,
+    n2_t,
+    out_acc,
+    dn2_acc,
+    act,
+    dup,
+    dmixed,
+    dtri,
+    carry,
+    vec_acc,
+    bup_acc,
+    vec_mine,
+    vec_t,
+    vec_sum,
+    vec_dp,
+    m_own,
+    m_core,
+    m_x,
+    m_y,
+    m_z,
+    q_own,
+    q_core,
+    q_x,
+    q_y,
+    q_z,
+    out_b,
+    gtok_b,
+    local_sem,
+    send_sem,
+    recv_sem,
+):
+    n_t, n_dp, rows, width, heads_w, hidden_w = sizes
+    n_y, n_x, n_z = n_t // CORES, WIDE, n_dp // WIDE
+    blocks = rows // BLOCK
+    d, t = lax.axis_index("dp"), lax.axis_index("tensor")
+    y, c = t // CORES, lax.rem(t, CORES)
+    z, x = d // WIDE, lax.rem(d, WIDE)
+
+    def t_peer(dy_, dc_):
+        return (d, lax.rem(y + dy_, n_y) * CORES + lax.rem(c + dc_, CORES))
+
+    def x_peer(k):
+        return (z * WIDE + lax.rem(x + k, n_x), t)
+
+    def z_peer(k):
+        return (lax.rem(z + k, n_z) * WIDE + x, t)
+
+    peers = [t_peer(s // CORES, s % CORES) for s in range(1, n_t)]
+    peers += [(lax.rem(d + k, n_dp), t) for k in range(1, n_dp)]
+    core = t_peer(0, 1)
+
+    barrier = pltpu.get_barrier_semaphore()
+    for peer in peers:
+        pl.semaphore_signal(barrier, inc=1, device_id=peer, device_id_type=MESH)
+
+    def local(src, dst, at):
+        copy = pltpu.make_async_copy(src, dst, local_sem.at[at])
+        copy.start()
+        return copy
+
+    load_tok = local(tok_h, tok, 0)
+    load_wq = local(wq_h, wq.at[0], 1)
+    load_wp = local(wp_h, wp.at[0], 2)
+    load_dy = local(dy_h, dy, 3)
+    load_wu = local(wu_h, wu.at[0], 4)
+    load_wd = local(wd_h, wd.at[0], 5)
+    bu[0] = jnp.broadcast_to(bu_ref[...], bu.shape[1:])
+    pl.semaphore_wait(barrier, len(peers))
+
+    copies = Copies(send_sem, recv_sem)
+
+    full = {"wq": (wq_h, wq), "wp": (wp_h, wp), "wu": (wu_h, wu), "wd": (wd_h, wd)}
+
+    def piece(ref, which):
+        part = ref.shape[0] // n_x
+        return ref.at[pl.ds(pl.multiple_of(which * part, part), part)]
+
+    def gather_send(name):
+        src, dst = full[name]
+        for k in range(1, n_y):
+            copies.start(
+                (name, "y", k), piece(src, x), piece(dst.at[CORES * k], x), t_peer(n_y - k, 0)
+            )
+        copies.start((name, "core", 0), src, dst.at[1], core)
+
+    def gather_first(name):
+        _, dst = full[name]
+        for k in range(1, n_y):
+            mine = piece(dst.at[CORES * k], x)
+            copies.arrived((name, "y", k), mine, core)
+            for j in range(1, n_x):
+                copies.start((name, "x", k, j), mine, mine, x_peer(j))
+            copies.start((name, "core", k, 0), mine, piece(dst.at[CORES * k + 1], x), core)
+
+    def gather_second(name):
+        _, dst = full[name]
+        for k in range(1, n_y):
+            for j in range(1, n_x):
+                which = lax.rem(x + n_x - j, n_x)
+                got = piece(dst.at[CORES * k], which)
+                copies.arrived((name, "x", k, j), got, core)
+                copies.start(
+                    (name, "core", k, j), got, piece(dst.at[CORES * k + 1], which), core
+                )
+
+    def gather_wait(name, s):
+        _, dst = full[name]
+        if s == 1:
+            copies.arrived((name, "core", 0), dst.at[1], core)
+        elif s % CORES == 1:
+            for j in range(n_x):
+                which = lax.rem(x + n_x - j, n_x)
+                copies.arrived((name, "core", s // CORES, j), piece(dst.at[s], which), core)
+
+    gather_send("wq")
+    for s in range(1, n_t):
+        copies.start(
+            ("bu", s),
+            bu.at[0],
+            bu.at[s],
+            t_peer((n_y - s // CORES) % n_y, (CORES - s % CORES) % CORES),
+        )
+
+    ln1_gain, ln1_bias = vecs_ref[0:1, :], vecs_ref[1:2, :]
+    proj_bias = vecs_ref[2:3, :]
+    ln2_gain, ln2_bias = vecs_ref[3:4, :], vecs_ref[4:5, :]
+    down_bias = vecs_ref[5:6, :]
+    vec_acc[...] = jnp.zeros_like(vec_acc)
+    bup_acc[...] = jnp.zeros_like(bup_acc)
+
+    clip = clip_ref[pl.ds(t, 1), :].astype(F32)
+    key_at = lax.broadcasted_iota(jnp.int32, (BLOCK, BLOCK), 0)
+    query_at = lax.broadcasted_iota(jnp.int32, (BLOCK, BLOCK), 1)
+    before = jnp.full((BLOCK, BLOCK), -1.0, F32)
+    for i in range(blocks):
+        row = clip[:, i * BLOCK : (i + 1) * BLOCK]
+        ids = jnp.broadcast_to(row, (BLOCK, BLOCK))
+        down = ids.T
+        bias[i, 0:BLOCK, :] = jnp.where(before == ids, 0.0, -1e30)
+        bias[i, BLOCK:, :] = jnp.where((down == ids) & (key_at <= query_at), 0.0, -1e30)
+        before = down
+
+    for s in range(n_t):
+        ks[s, 0:BLOCK, :] = jnp.zeros((BLOCK, heads_w), BF)
+        vs[s, 0:BLOCK, :] = jnp.zeros((BLOCK, heads_w), BF)
+        ks_t[s, :, 0:BLOCK] = jnp.zeros((heads_w, BLOCK), BF)
+        vs_t[s, :, 0:BLOCK] = jnp.zeros((heads_w, BLOCK), BF)
+
+    def at(i, size, offset=0):
+        return pl.ds(pl.multiple_of(i * size + offset, math.gcd(size, offset) if offset else size), size)
+
+    load_tok.wait()
+
+    @pl.loop(0, rows // ROWS)
+    def _(i):
+        here = at(i, ROWS)
+        v = tok[here, :].astype(F32)
+        mean = jnp.mean(v, axis=-1, keepdims=True)
+        centre = v - mean
+        r = lax.rsqrt(jnp.mean(centre * centre, axis=-1, keepdims=True) + epsilon)
+        normed = (centre * r * ln1_gain + ln1_bias).astype(BF)
+        n1[here, :] = normed
+        n1_t[:, here] = normed.T
+        stats[0, here, :] = jnp.broadcast_to(mean, (ROWS, BLOCK))
+        stats[1, here, :] = jnp.broadcast_to(r, (ROWS, BLOCK))
+
+    first_head = lax.broadcasted_iota(jnp.int32, (BLOCK, heads_w), 1) < HD
+
+    def two_heads(block):
+        zero = jnp.zeros_like(block)
+        return jnp.concatenate(
+            [jnp.where(first_head, block, zero), jnp.where(first_head, zero, block)], axis=0
+        )
+
+    def pick_heads(both):
+        own = jnp.concatenate([both[:HD, :BLOCK], both[HD:, BLOCK:]], axis=0)
+        return own.T
+
+    def project_heads(s):
+        @pl.loop(0, rows // ROWS)
+        def _(i):
+            here = at(i, ROWS)
+            got = mm(n1[here, :], wq[s])
+            qs[s, here, :] = got[:, :heads_w].astype(BF) * jnp.asarray(HD**-0.5, BF)
+            k = got[:, heads_w : 2 * heads_w].astype(BF)
+            v = got[:, 2 * heads_w :].astype(BF)
+            there = at(i, ROWS, BLOCK)
+            ks[s, there, :] = k
+            vs[s, there, :] = v
+            ks_t[s, :, there] = k.T
+            vs_t[s, :, there] = v.T
+
+    def attend_slot(s):
+        @pl.loop(0, blocks)
+        def _(i):
+            here = at(i, BLOCK)
+            seen = pl.ds(pl.multiple_of(i * BLOCK, BLOCK), 2 * BLOCK)
+            one = bias[i]
+            scores = mm_nt(ks[s, seen, :], two_heads(qs[s, here, :]))
+            scores = scores + jnp.concatenate([one, one], axis=1)
+            peak = jnp.max(scores, axis=0, keepdims=True)
+            expo = jnp.exp(scores - peak)
+            total = jnp.sum(expo, axis=0, keepdims=True)
+            low = (expo * (1.0 / total)).astype(BF)
+            probs[s, i] = low
+            mixed[here, s * heads_w : (s + 1) * heads_w] = pick_heads(
+                mm(vs_t[s, :, seen], low)
+            ).astype(BF)
+
+    load_wq.wait()
+    project_heads(0)
+    attend_slot(0)
+    gather_first("wq")
+    gather_send("wp")
+    gather_send("wu")
+    gather_wait("wq", 1)
+    project_heads(1)
+    attend_slot(1)
+    gather_second("wq")
+    for s in range(2, n_t):
+        if s == 3:
+            gather_first("wp")
+            gather_first("wu")
+            gather_send("wd")
+        gather_wait("wq", s)
+        project_heads(s)
+        attend_slot(s)
+    gather_second("wp")
+    gather_second("wu")
+
+    load_wp.wait()
+    load_dy.wait()
+    for s in range(1, n_t):
+        gather_wait("wp", s)
+
+    @pl.loop(0, rows // ROWS)
+    def _(i):
+        here = at(i, ROWS)
+        v = tok[here, :].astype(F32) + proj_bias
+        v = v + mm(mixed[here, :], wp[...].reshape(n_t * heads_w, width))
+        hidden[here, :] = v
+        mean = jnp.mean(v, axis=-1, keepdims=True)
+        centre = v - mean
+        r = lax.rsqrt(jnp.mean(centre * centre, axis=-1, keepdims=True) + epsilon)
+        normed = (centre * r * ln2_gain + ln2_bias).astype(BF)
+        n2[here, :] = normed
+        n2_t[:, here] = normed.T
+        stats[2, here, :] = jnp.broadcast_to(mean, (ROWS, BLOCK))
+        stats[3, here, :] = jnp.broadcast_to(r, (ROWS, BLOCK))
+        dy_t[:, here] = dy[here, :].T
+
+    def mlp_slot(s):
+        @pl.loop(0, rows // ROWS)
+        def _(i):
+            here = at(i, ROWS)
+            u = mm(n2[here, :], wu[s]) + bu[s, 0:1, :]
+            dact = mm_nt(dy[here, :], wd[s])
+            cdf, bell = normal_parts(u)
+            active = (u * cdf).astype(BF)
+            du = (dact * (cdf + bell)).astype(BF)
+            act[here, :] = active
+            dup[here, :] = du
+            bup_acc[s] += by_eight(du.astype(F32))
+            up_part = mm(active, wd[s])
+            back_part = mm_nt(du, wu[s])
+            if s == 0:
+                out_acc[here, :] = up_part
+                dn2_acc[here, :] = back_part
+            else:
+                out_acc[here, :] += up_part
+                dn2_acc[here, :] += back_part
+
+        tile = 2 * n_x * m_own.shape[3]
+
+        @pl.loop(0, width // tile)
+        def _(j):
+            here = at(j, tile)
+            split = (2, n_x, m_own.shape[3], hidden_w)
+            m_own[s, pl.ds(2 * j, 2), :, :, 0:hidden_w] = (
+                mm(n2_t[here, :], dup[...]).astype(BF).reshape(split)
+            )
+            m_own[s, pl.ds(2 * j, 2), :, :, hidden_w:] = (
+                mm(dy_t[here, :], act[...]).astype(BF).reshape(split)
+            )
+
+    def rs_core_send(tag, own, got, k):
+        copies.start((tag, "c", k), own.at[CORES * k + 1], got.at[k], core)
+
+    def rs_x_send(tag, own, got, after, k):
+        copies.arrived((tag, "c", k), got.at[k], core)
+
+        @pl.loop(0, n_z)
+        def _(a):
+            own[CORES * k, a] = own[CORES * k, a] + got[k, a]
+
+        for j in range(1, n_x):
+            which = lax.rem(x + j, n_x)
+            copies.start(
+                (tag, "x", k, j), own.at[CORES * k, :, which], after.at[k, j - 1], x_peer(j)
+            )
+
+    def rs_x_sum(tag, own, after, k):
+        for j in range(1, n_x):
+            copies.arrived((tag, "x", k, j), after.at[k, j - 1], core)
+
+        @pl.loop(0, n_z)
+        def _(a):
+            total = own[CORES * k, a, x].astype(F32)
+            for j in range(1, n_x):
+                total = total + after[k, j - 1, a].astype(F32)
+            after[k, 0, a] = total.astype(BF)
+
+    def rs_y_send(tag, after, got, k):
+        copies.start((tag, "y", k), after.at[k, 0], got.at[k - 1], t_peer(k, 0))
+
+    def rs_z_send(tag, after, got, last):
+        for k in range(1, n_y):
+            copies.arrived((tag, "y", k), got.at[k - 1], core)
+
+        @pl.loop(0, n_z)
+        def _(a):
+            total = after[0, 0, a].astype(F32)
+            for k in range(1, n_y):
+                total = total + got[k - 1, a].astype(F32)
+            after[0, 0, a] = total.astype(BF)
+
+        for k in range(1, n_z):
+            copies.start(
+                (tag, "z", k), after.at[0, 0, lax.rem(z + k, n_z)], last.at[k - 1], z_peer(k)
+            )
+
+    def rs_finish(tag, after, last, result):
+        for k in range(1, n_z):
+            copies.arrived((tag, "z", k), last.at[k - 1], core)
+        total = after[0, 0, z].astype(F32)
+        for k in range(1, n_z):
+            total = total + last[k - 1].astype(F32)
+        result[...] = total
+
+    load_wu.wait()
+    load_wd.wait()
+    for s in range(1, n_t):
+        copies.arrived(("bu", s), bu.at[s], core)
+    gather_first("wd")
+    mlp_slot(0)
+    gather_second("wd")
+    for s in range(1, n_t):
+        gather_wait("wu", s)
+        gather_wait("wd", s)
+        mlp_slot(s)
+        if s % CORES == 1:
+            rs_core_send("m", m_own, m_core, s // CORES)
+        elif s >= 2:
+            rs_x_send("m", m_own, m_core, m_x, s // CORES - 1)
+    rs_x_send("m", m_own, m_core, m_x, n_y - 1)
+
+    @pl.loop(0, rows // ROWS)
+    def _(i):
+        here = at(i, ROWS)
+        value = hidden[here, :]
+        out_b[here, :] = (value + out_acc[here, :] + down_bias).astype(BF)
+        mean = stats[2, here, 0:1]
+        r = stats[3, here, 0:1]
+        xhat = (value - mean) * r
+        dn = dn2_acc[here, :]
+        g = dy[here, :].astype(F32)
+        scaled = dn * ln2_gain
+        first = jnp.mean(scaled, axis=-1, keepdims=True)
+        second = jnp.mean(scaled * xhat, axis=-1, keepdims=True)
+        dh = g + r * (scaled - first - xhat * second)
+        hidden[here, :] = dh
+        low = dh.astype(BF)
+        dy_t[:, here] = low.T
+        dmixed[here, :] = mm_nt(low, wp[...].reshape(n_t * heads_w, width)).astype(BF)
+        vec_acc[2] += by_eight(dh)
+        vec_acc[3] += by_eight(dn * xhat)
+        vec_acc[4] += by_eight(dn)
+        vec_acc[5] += by_eight(g)
+
+    store_out = local(out_b, out_h, 6)
+
+    qkv_w = 3 * heads_w
+    tile = 2 * n_x * q_own.shape[3]
+
+    @pl.loop(0, width // tile)
+    def _(j):
+        got = mm(dy_t[at(j, tile), :], mixed[...]).astype(BF)
+        for s in range(n_t):
+            q_own[s, pl.ds(2 * j, 2), :, :, qkv_w:] = got[
+                :, s * heads_w : (s + 1) * heads_w
+            ].reshape(2, n_x, q_own.shape[3], heads_w)
+
+    def attend_back_slot(s):
+        carry[...] = jnp.zeros_like(carry)
+
+        @pl.loop(0, blocks)
+        def _(i):
+            here = at(i, BLOCK)
+            seen = pl.ds(pl.multiple_of(i * BLOCK, BLOCK), 2 * BLOCK)
+            grad = two_heads(dmixed[here, s * heads_w : (s + 1) * heads_w])
+            low = probs[s, i]
+            p = low.astype(F32)
+            weighed = p * mm_nt(vs[s, seen, :], grad)
+            ds = (weighed - p * jnp.sum(weighed, axis=0, keepdims=True)).astype(BF)
+            dv = mm(low, grad)
+            dk = mm(ds, two_heads(qs[s, here, :]))
+            dq = pick_heads(mm(ks_t[s, :, seen], ds)) * (HD**-0.5)
+            dtri[s, at(i, BLOCK, BLOCK), 0:heads_w] = dq.astype(BF)
+            dtri[s, here, heads_w : 2 * heads_w] = (carry[0] + dk[:BLOCK]).astype(BF)
+            dtri[s, here, 2 * heads_w :] = (carry[1] + dv[:BLOCK]).astype(BF)
+            carry[0] = dk[BLOCK:]
+            carry[1] = dv[BLOCK:]
+
+        dtri[s, rows:, heads_w : 2 * heads_w] = carry[0].astype(BF)
+        dtri[s, rows:, 2 * heads_w :] = carry[1].astype(BF)
+
+        @pl.loop(0, width // tile)
+        def _(j):
+            q_own[s, pl.ds(2 * j, 2), :, :, 0:qkv_w] = (
+                mm(n1_t[at(j, tile), :], dtri[s, BLOCK:, :])
+                .astype(BF)
+                .reshape(2, n_x, q_own.shape[3], qkv_w)
+            )
+
+    for k in reversed(range(n_y)):
+        attend_back_slot(CORES * k + 1)
+        rs_core_send("q", q_own, q_core, k)
+        rs_x_sum("m", m_own, m_x, k)
+        if k > 0:
+            rs_y_send("m", m_x, m_y, k)
+        if k < n_y - 1:
+            rs_x_sum("q", q_own, q_x, k + 1)
+            rs_y_send("q", q_x, q_y, k + 1)
+        attend_back_slot(CORES * k)
+        rs_x_send("q", q_own, q_core, q_x, k)
+    rs_z_send("m", m_x, m_y, m_z)
+
+    @pl.loop(0, rows // ROWS)
+    def _(i):
+        here = at(i, ROWS)
+        there = at(i, ROWS, BLOCK)
+        dn = mm_nt(dtri[0, there, :], wq[0])
+        for s in range(1, n_t):
+            dn = dn + mm_nt(dtri[s, there, :], wq[s])
+        mean = stats[0, here, 0:1]
+        r = stats[1, here, 0:1]
+        xhat = (tok[here, :].astype(F32) - mean) * r
+        scaled = dn * ln1_gain
+        first = jnp.mean(scaled, axis=-1, keepdims=True)
+        second = jnp.mean(scaled * xhat, axis=-1, keepdims=True)
+        gtok_b[here, :] = (hidden[here, :] + r * (scaled - first - xhat * second)).astype(BF)
+        vec_acc[0] += by_eight(dn * xhat)
+        vec_acc[1] += by_eight(dn)
+
+    store_gtok = local(gtok_b, gtok_h, 7)
+
+    for s in range(n_t):
+        lines = [jnp.sum(vec_acc[k], axis=0, keepdims=True) for k in range(6)]
+        lines.append(jnp.sum(bup_acc[s], axis=0, keepdims=True))
+        lines.append(jnp.zeros((1, width), F32))
+        vec_mine[s] = jnp.concatenate(lines, axis=0)
+    for s in range(1, n_t):
+        copies.start(
+            ("vt", s), vec_mine.at[s], vec_t.at[s - 1], t_peer(s // CORES, s % CORES)
+        )
+    rs_x_sum("q", q_own, q_x, 0)
+    rs_z_send("q", q_x, q_y, q_z)
+    total = vec_mine[0]
+    for s in range(1, n_t):
+        copies.arrived(("vt", s), vec_t.at[s - 1], core)
+        total = total + vec_t[s - 1]
+    vec_sum[...] = total
+    for k in range(1, n_dp):
+        copies.start(("vd", k), vec_sum, vec_dp.at[k - 1], (lax.rem(d + k, n_dp), t))
+    rs_finish("m", m_x, m_z, gm_ref)
+    for k in range(1, n_dp):
+        copies.arrived(("vd", k), vec_dp.at[k - 1], core)
+        total = total + vec_dp[k - 1]
+    gv_ref[...] = total
+    rs_finish("q", q_x, q_z, gq_ref)
+    store_out.wait()
+    store_gtok.wait()
+    copies.drain()
+
+
+def fused_device(
+    n_t,
+    n_dp,
+    tokens,
+    clip_ids,
+    ln1_gain,
+    ln1_bias,
+    query_key_value_weight,
+    projection_weight,
+    attention_output_bias,
+    ln2_gain,
+    ln2_bias,
+    up_weight,
+    mlp_up_bias,
+    down_weight,
+    mlp_down_bias,
+    grad_output,
+):
+    _, rows, width = tokens.shape
+    heads_w = projection_weight.shape[0]
+    hidden_w = up_weight.shape[1]
+    n_y, n_x, n_z = n_t // CORES, WIDE, n_dp // WIDE
+    part = width // n_dp
+    blocks = rows // BLOCK
+    qkv_w = 3 * heads_w
+    vecs = jnp.stack(
+        [ln1_gain, ln1_bias, attention_output_bias, ln2_gain, ln2_bias, mlp_down_bias]
+    )
+
+    def chunk(w):
+        return [
+            pltpu.VMEM((n_t, n_z, n_x, part, w), BF),
+            pltpu.VMEM((n_y, n_z, n_x, part, w), BF),
+            pltpu.VMEM((n_y, n_x - 1, n_z, part, w), BF),
+            pltpu.VMEM((n_y - 1, n_z, part, w), BF),
+            pltpu.VMEM((n_z - 1, part, w), BF),
+        ]
+
+    def half(*shape):
+        return pltpu.VMEM(shape, BF)
+
+    def single(*shape):
+        return pltpu.VMEM(shape, F32)
+
+    scratch = [
+        half(rows, width),
+        half(rows, width),
+        half(width, rows),
+        half(n_t, width, qkv_w),
+        half(n_t, heads_w, width),
+        half(n_t, width, hidden_w),
+        half(n_t, hidden_w, width),
+        single(n_t, 8, hidden_w),
+        half(rows, width),
+        half(width, rows),
+        single(4, rows, BLOCK),
+        half(n_t, rows, heads_w),
+        half(n_t, rows + BLOCK, heads_w),
+        half(n_t, rows + BLOCK, heads_w),
+        half(n_t, heads_w, rows + BLOCK),
+        half(n_t, heads_w, rows + BLOCK),
+        single(blocks, 2 * BLOCK, BLOCK),
+        half(n_t, blocks, 2 * BLOCK, 2 * BLOCK),
+        half(rows, n_t * heads_w),
+        single(rows, width),
+        half(rows, width),
+        half(width, rows),
+        single(rows, width),
+        single(rows, width),
+        half(rows, hidden_w),
+        half(rows, hidden_w),
+        half(rows, n_t * heads_w),
+        half(n_t, rows + BLOCK, qkv_w),
+        single(2, BLOCK, heads_w),
+        single(6, 8, width),
+        single(n_t, 8, hidden_w),
+        single(n_t, 8, width),
+        single(n_t - 1, 8, width),
+        single(8, width),
+        single(n_dp - 1, 8, width),
+        *chunk(2 * hidden_w),
+        *chunk(qkv_w + heads_w),
+        half(rows, width),
+        half(rows, width),
+        pltpu.SemaphoreType.DMA((8,)),
+        pltpu.SemaphoreType.DMA((64,)),
+        pltpu.SemaphoreType.DMA((64,)),
+    ]
+    anywhere = pl.BlockSpec(memory_space=pl.ANY)
+    near = pl.BlockSpec(memory_space=pltpu.VMEM)
+    out, gtok, gm, gq, gv = pl.pallas_call(
+        functools.partial(layer_kernel, (n_t, n_dp, rows, width, heads_w, hidden_w)),
+        out_shape=(
+            jax.ShapeDtypeStruct((rows, width), BF),
+            jax.ShapeDtypeStruct((rows, width), BF),
+            jax.ShapeDtypeStruct((part, 2 * hidden_w), F32),
+            jax.ShapeDtypeStruct((part, qkv_w + heads_w), F32),
+            jax.ShapeDtypeStruct((8, width), F32),
+        ),
+        in_specs=[anywhere, anywhere, near, near, near] + [anywhere] * 4,
+        out_specs=(anywhere, anywhere, near, near, near),
+        scratch_shapes=scratch,
+        compiler_params=pltpu.CompilerParams(
+            collective_id=0, has_side_effects=True, vmem_limit_bytes=63 << 20
+        ),
+    )(
+        tokens.reshape(rows, width),
+        grad_output.reshape(rows, width),
+        clip_ids,
+        vecs,
+        mlp_up_bias.reshape(1, hidden_w),
+        query_key_value_weight.reshape(width, qkv_w),
+        projection_weight,
+        up_weight,
+        down_weight,
+    )
+    d, t = lax.axis_index("dp"), lax.axis_index("tensor")
+    share = width // (n_dp * n_t)
+    vectors = lax.dynamic_slice(gv, (0, (d * n_t + t) * share), (6, share))
+    g_up_bias = lax.dynamic_slice(gv, (6, d * (hidden_w // n_dp)), (1, hidden_w // n_dp))
+    return (
+        out[None],
+        gtok[None],
+        vectors[0],
+        vectors[1],
+        gq[:, :qkv_w].reshape(part, 3, heads_w),
+        gq[:, qkv_w:].T,
+        vectors[2],
+        vectors[3],
+        vectors[4],
+        gm[:, :hidden_w],
+        g_up_bias,
+        gm[:, hidden_w:].T,
+        vectors[5],
+    )
+
+
+def fits(mesh, shapes):
+    n_t, n_dp = mesh.shape["tensor"], mesh.shape["dp"]
+    seqs, length, width = shapes[0]
+    features = shapes[4][2] // n_t
+    hidden_w = shapes[9][1] // n_t
+    return (
+        seqs == n_t * n_dp
+        and length % ROWS == 0
+        and features == 2 * HD == BLOCK
+        and hidden_w == width
+        and n_t % CORES == 0
+        and n_t // CORES > 1
+        and n_dp % (2 * WIDE) == 0
+        and (width // n_dp) % 16 == 0
+    )
+
+
 def solution(mesh):
     in_specs = (
         P(("dp", "tensor"), None, None),
@@ -292,6 +1036,13 @@
         P("tensor", "dp"),
         P(("dp", "tensor")),
     )
-    return jax.shard_map(
-        on_device, mesh=mesh, in_specs=in_specs, out_specs=out_specs, check_vma=False
-    )
+
+    def run(*arrays):
+        body = on_device
+        if fits(mesh, [a.shape for a in arrays]):
+            body = functools.partial(fused_device, mesh.shape["tensor"], mesh.shape["dp"])
+        return jax.shard_map(
+            body, mesh=mesh, in_specs=in_specs, out_specs=out_specs, check_vma=False
+        )(*arrays)
+
+    return run

time: 814 us -> 131 us (0.16); the launches traced: 804 us -> 130 us
  waiting for transfers between devices: 478 us -> 0 us
  matrix products: 143 us -> 0 us
  Pallas kernels: 0 us -> 117 us
  other arithmetic: 83.4 us -> 0 us
  blocking collectives: 39.5 us -> 0 us
  local copies, waits for them, and re-layouts: 30.6 us -> 12.3 us
  starting transfers between devices: 14 us -> 0 us
  between operations: 14.7 us -> 0.73 us
    reduce_scatter x8 -> x0, waiting for transfers between devices: 382 us -> none  [the longest x1 63.9 us: on_device(): lax.psum_scatter(query_key_value_gradient.astype(jnp.bfloat16), 'dp', sca...]
    dot_general x68 -> x0, matrix products: 143 us -> none  [the longest x16 32.4 us: block_scores(): jnp.einsum('qhd,khd->hqk', query[start:start + block], keys, preferred_el...]
    pallas_call x0 -> x1, Pallas kernels: none -> 117 us  [fused_device(): pl.pallas_call(functools.partial(layer_kernel, (n_t, n_dp, rows, width, h...]
    all_gather x4 -> x0, waiting for transfers between devices: 95.1 us -> none  [the longest x1 37.3 us: on_device(): lax.all_gather(first_normalized, 'tensor', axis=0, tiled=True)]
    unnamed x1 -> x0, blocking collectives: 39.5 us -> none
    convert_element_type x18 -> x0, other arithmetic: 38.5 us -> none  [the longest x1 20.4 us: on_device(): active_rows_now = gelu_exact(upper_half_rows).astype(jnp.bfloat16)]
    reduce_sum x13 -> x0, other arithmetic: 29.6 us -> none  [the longest x4 9.67 us: attend_sequence(): total = jnp.sum(expo, axis=-1, keepdims=True)]
    all_gather x4 -> x0, starting transfers between devices: 13.1 us -> none  [the longest x1 13 us: on_device(): branch_every_row = lax.all_gather(branch_low, 'tensor', axis=0, tiled=True)]
  transfers between devices with their start and end apart: 13 -> 0, of which waited for: 12 -> 0; matrix products, arithmetic and copies ran while one was open for 18% -> 0% of each run, Pallas kernels for 0% -> 0%
where the time goes in v1:
time: 131 us; the launch traced here: 130 us
  Pallas kernels  117 us (89%)
  local copies, waits for them, and re-layouts  12.3 us (9%)
    pallas_call x1, Pallas kernels, fused_device(): pl.pallas_call(functools.partial(layer_kernel, (n_t, n_dp, rows, width, h...  117 us
    unnamed x20, local copies, waits for them, and re-layouts  5.83 us

profile of v1, /device:TPU:0, one launch (start us, length us, event | category | flops | bytes accessed | tf_op | source)
XLA Modules:
  0.0 130.4 jit_solution(3446584756223826615)
XLA Ops:
  0.7 1.2 copy.29
  1.8 0.0 copy-start.4
  1.8 0.0 copy-start.5
  1.8 0.0 copy-start.6
  1.9 0.0 copy-start.7
  1.9 0.9 copy.30.wq_h
  2.8 0.0 copy-start.3
  2.8 0.0 copy-start.2
  2.8 0.0 copy-done.4
  2.8 0.0 copy-done.5
  2.8 0.0 copy-done.6
  2.8 0.0 copy-done.7
  2.8 0.6 copy-done.3
  3.5 0.0 copy-done.2
  3.5 0.6 stack.27.vecs_ref
  4.1 117.4 %shard_map.237 = (bf16[1024,512]{1,0:T(8,128)(2,1)}, bf16[1024,512]{1,0:T(8,128)(2,1)}, f32[64,1024]{1,0:T(8,128)}, f32[64,512]{1,0:T(8,128)}, f32[8,512]{1,0:T(8,128)}) custom-call(bf16[1024,512]{1,0:T(8,128)(2,1)} %bitcast.34, bf16[1024,512]{1,0:T(8,128)(2,1)} %bitcast.35, s32[4,1024]{1,0:T(4,128)} %clip_ref.1, f32[6,512]{1,0:T(8,128)} %stack.27.vecs_ref, ...), custom_call_target="tpu_custom_call" | custom-call | tf_op jit(solution)/shard_map/pallas_call | solution.py:943
  121.5 0.7 constant_dynamic-slice_fusion.1
  122.2 0.5 slice_bitcast_fusion.3
  122.8 1.3 constant_dynamic-slice_fusion
  124.0 0.0 copy-start.1
  124.0 1.7 %slice_bitcast_fusion = (f32[512,64]{0,1:T(8,128)}, f32[64,512]{1,0:T(8,128)}) fusion(f32[64,1024]{1,0:T(8,128)} %get-tuple-element.22), kind=kLoop, calls=%fused_computation | loop fusion | bytes 524288 | tf_op jit(solution)/shard_map/transpose | solution.py:985
  125.8 0.0 copy-done.1
  125.8 0.6 copy_bitcast_fusion
  126.4 0.6 slice_bitcast_fusion.2
  127.0 0.0 copy-start
  127.0 2.4 %copy.36 = bf16[1,1024,512]{2,1,0:T(8,128)(2,1)} copy(bf16[1,1024,512]{2,1,0:T(8,128)(2,1)} %bitcast.37) | data formatting | bytes 2097152
  129.4 0.0 copy-done
  129.4 1.0 copy.37
Async XLA Ops:
  1.8 1.0 copy-start.4
  1.8 1.0 copy-start.5
  1.8 1.0 copy-start.6
  1.9 1.0 copy-start.7
  2.8 0.7 copy-start.3
  2.8 0.7 copy-start.2
  124.0 1.7 %copy-start.1 = (f32[64,512]{1,0:T(8,128)S(1)}, f32[64,512]{1,0:T(8,128)}, u32[]{:S(2)}) copy-start(f32[64,512]{1,0:T(8,128)} %get-tuple-element.21) | copy-start | bytes 393220
  127.0 2.4 %copy-start = (bf16[1024,512]{1,0:T(8,128)(2,1)S(1)}, bf16[1024,512]{1,0:T(8,128)(2,1)}, u32[]{:S(2)}) copy-start(bf16[1024,512]{1,0:T(8,128)(2,1)} %get-tuple-element.19) | copy-start | bytes 3145732

commit v2 on v1

--- a/solution.py
+++ b/solution.py
@@ -11,6 +11,7 @@
 HD = 64
 CORES = 2
 WIDE = 2
+PAIR = 2
 BF = jnp.bfloat16
 F32 = jnp.float32
 MESH = pl.DeviceIdType.MESH
@@ -272,6 +273,35 @@
 
 BLOCK = 128
 ROWS = 256
+WIDE_ROWS = 512
+
+ORDER = {"u": "xylh", "d": "lxyh", "p": "xylh", "qk": "xylh", "v": "lyxh"}
+SCHEDULE = {
+    "start": ("wq", "wp",),
+    "heads0": ("wq",),
+    "attend0": ("wp", "wd", "wq", "wu",),
+    "attend1": ("wq", "wp",),
+    "heads2": ("wd",),
+    "attend2": ("wp",),
+    "hidden": ("wu",),
+    "mlp1": ("wd",),
+    "rows0.0": ("wu", "d0",),
+    "rows0.1": ("u0", "wd",),
+    "mlp0": ("wu", "d0", "u0",),
+    "rows2.1": ("d1", "d0", "u0", "u1",),
+    "mlp2": ("u1", "d1",),
+    "proj": ("p1",),
+    "back3": ("p0", "p1", "d0",),
+    "qkv3": ("qk1", "p0", "u1",),
+    "back2": ("d1",),
+    "qkv2": ("qk1",),
+    "back1": ("v1", "p1", "p0",),
+    "qkv1": ("qk0", "v1", "v0", "d1",),
+    "back0": ("p", "qk1", "u", "v1",),
+    "qkv0": ("qk0", "v0", "p", "d",),
+    "norm1.1": ("vec", "qk0", "qk", "u", "v0", "v", "v", "p",),
+    "end": ("vec", "qk", "v", "u", "d", "vec", "qk",),
+}
 
 
 def mm(left, right):
@@ -282,18 +312,13 @@
     return lax.dot_general(left, right, (((1,), (1,)), ((), ())), preferred_element_type=F32)
 
 
+def mm_tn(left, right):
+    return lax.dot_general(left, right, (((0,), (0,)), ((), ())), preferred_element_type=F32)
+
+
 def normal_parts(u):
+    cdf = 0.5 + 0.5 * lax.erf(u * math.sqrt(0.5))
     bell = jnp.exp2(u * u * (-0.5 * math.log2(math.e)))
-    base = 1.0 + jnp.abs(u) * (0.3275911 * math.sqrt(0.5))
-    t = pl.reciprocal(base, approx=True)
-    t = t * (2.0 - base * t)
-    poly = 0.5 * 1.061405429
-    poly = poly * t - 0.5 * 1.453152027
-    poly = poly * t + 0.5 * 1.421413741
-    poly = poly * t - 0.5 * 0.284496736
-    poly = poly * t + 0.5 * 0.254829592
-    half = poly * t * bell
-    cdf = jnp.where(u >= 0.0, 1.0 - half, half)
     return cdf, u * bell * (1.0 / math.sqrt(2.0 * math.pi))
 
 
@@ -334,7 +359,12 @@
     tok_h,
     dy_h,
     clip_ref,
-    vecs_ref,
+    ln1_gain_ref,
+    ln1_bias_ref,
+    proj_bias_ref,
+    ln2_gain_ref,
+    ln2_bias_ref,
+    down_bias_ref,
     bu_ref,
     wq_h,
     wp_h,
@@ -342,19 +372,19 @@
     wd_h,
     out_h,
     gtok_h,
-    gm_ref,
     gq_ref,
+    gp_ref,
+    gu_ref,
+    gd_ref,
     gv_ref,
     tok,
     dy,
-    dy_t,
     wq,
     wp,
     wu,
     wd,
     bu,
     n1,
-    n1_t,
     stats,
     qs,
     ks,
@@ -366,30 +396,24 @@
     mixed,
     hidden,
     n2,
-    n2_t,
     out_acc,
     dn2_acc,
     act,
     dup,
+    branch,
     dmixed,
     dtri,
-    carry,
     vec_acc,
     bup_acc,
     vec_mine,
     vec_t,
     vec_sum,
     vec_dp,
-    m_own,
-    m_core,
-    m_x,
-    m_y,
-    m_z,
-    q_own,
-    q_core,
-    q_x,
-    q_y,
-    q_z,
+    u_bufs,
+    d_bufs,
+    p_bufs,
+    qk_bufs,
+    v_bufs,
     out_b,
     gtok_b,
     local_sem,
@@ -397,11 +421,14 @@
     recv_sem,
 ):
     n_t, n_dp, rows, width, heads_w, hidden_w = sizes
-    n_y, n_x, n_z = n_t // CORES, WIDE, n_dp // WIDE
+    n_y, n_x, n_l, n_h = n_t // CORES, WIDE, PAIR, n_dp // (WIDE * PAIR)
     blocks = rows // BLOCK
+    part = width // n_dp
+    qkv_w = 3 * heads_w
     d, t = lax.axis_index("dp"), lax.axis_index("tensor")
     y, c = t // CORES, lax.rem(t, CORES)
     z, x = d // WIDE, lax.rem(d, WIDE)
+    z_far, z_near = z // n_l, lax.rem(z, n_l)
 
     def t_peer(dy_, dc_):
         return (d, lax.rem(y + dy_, n_y) * CORES + lax.rem(c + dc_, CORES))
@@ -409,8 +436,11 @@
     def x_peer(k):
         return (z * WIDE + lax.rem(x + k, n_x), t)
 
-    def z_peer(k):
-        return (lax.rem(z + k, n_z) * WIDE + x, t)
+    def l_peer(k):
+        return ((z_far * n_l + lax.rem(z_near + k, n_l)) * WIDE + x, t)
+
+    def h_peer(k):
+        return ((lax.rem(z_far + k, n_h) * n_l + z_near) * WIDE + x, t)
 
     peers = [t_peer(s // CORES, s % CORES) for s in range(1, n_t)]
     peers += [(lax.rem(d + k, n_dp), t) for k in range(1, n_dp)]
@@ -432,66 +462,11 @@
     load_wu = local(wu_h, wu.at[0], 4)
     load_wd = local(wd_h, wd.at[0], 5)
     bu[0] = jnp.broadcast_to(bu_ref[...], bu.shape[1:])
-    pl.semaphore_wait(barrier, len(peers))
-
-    copies = Copies(send_sem, recv_sem)
-
-    full = {"wq": (wq_h, wq), "wp": (wp_h, wp), "wu": (wu_h, wu), "wd": (wd_h, wd)}
-
-    def piece(ref, which):
-        part = ref.shape[0] // n_x
-        return ref.at[pl.ds(pl.multiple_of(which * part, part), part)]
-
-    def gather_send(name):
-        src, dst = full[name]
-        for k in range(1, n_y):
-            copies.start(
-                (name, "y", k), piece(src, x), piece(dst.at[CORES * k], x), t_peer(n_y - k, 0)
-            )
-        copies.start((name, "core", 0), src, dst.at[1], core)
-
-    def gather_first(name):
-        _, dst = full[name]
-        for k in range(1, n_y):
-            mine = piece(dst.at[CORES * k], x)
-            copies.arrived((name, "y", k), mine, core)
-            for j in range(1, n_x):
-                copies.start((name, "x", k, j), mine, mine, x_peer(j))
-            copies.start((name, "core", k, 0), mine, piece(dst.at[CORES * k + 1], x), core)
-
-    def gather_second(name):
-        _, dst = full[name]
-        for k in range(1, n_y):
-            for j in range(1, n_x):
-                which = lax.rem(x + n_x - j, n_x)
-                got = piece(dst.at[CORES * k], which)
-                copies.arrived((name, "x", k, j), got, core)
-                copies.start(
-                    (name, "core", k, j), got, piece(dst.at[CORES * k + 1], which), core
-                )
-
-    def gather_wait(name, s):
-        _, dst = full[name]
-        if s == 1:
-            copies.arrived((name, "core", 0), dst.at[1], core)
-        elif s % CORES == 1:
-            for j in range(n_x):
-                which = lax.rem(x + n_x - j, n_x)
-                copies.arrived((name, "core", s // CORES, j), piece(dst.at[s], which), core)
-
-    gather_send("wq")
-    for s in range(1, n_t):
-        copies.start(
-            ("bu", s),
-            bu.at[0],
-            bu.at[s],
-            t_peer((n_y - s // CORES) % n_y, (CORES - s % CORES) % CORES),
-        )
-
-    ln1_gain, ln1_bias = vecs_ref[0:1, :], vecs_ref[1:2, :]
-    proj_bias = vecs_ref[2:3, :]
-    ln2_gain, ln2_bias = vecs_ref[3:4, :], vecs_ref[4:5, :]
-    down_bias = vecs_ref[5:6, :]
+
+    ln1_gain, ln1_bias = ln1_gain_ref[...], ln1_bias_ref[...]
+    proj_bias = proj_bias_ref[...]
+    ln2_gain, ln2_bias = ln2_gain_ref[...], ln2_bias_ref[...]
+    down_bias = down_bias_ref[...]
     vec_acc[...] = jnp.zeros_like(vec_acc)
     bup_acc[...] = jnp.zeros_like(bup_acc)
 
@@ -527,9 +502,220 @@
         r = lax.rsqrt(jnp.mean(centre * centre, axis=-1, keepdims=True) + epsilon)
         normed = (centre * r * ln1_gain + ln1_bias).astype(BF)
         n1[here, :] = normed
-        n1_t[:, here] = normed.T
         stats[0, here, :] = jnp.broadcast_to(mean, (ROWS, BLOCK))
         stats[1, here, :] = jnp.broadcast_to(r, (ROWS, BLOCK))
+
+    pl.semaphore_wait(barrier, len(peers))
+    copies = Copies(send_sem, recv_sem)
+
+    full = {"wq": (wq_h, wq), "wp": (wp_h, wp), "wu": (wu_h, wu), "wd": (wd_h, wd)}
+
+    def rows_of(ref, which, parts):
+        part = ref.shape[-2] // parts
+        here = pl.ds(pl.multiple_of(which * part, part), part)
+        return ref.at[:, here] if len(ref.shape) == 3 else ref.at[here]
+
+    def gather(name):
+        src, dst = full[name]
+        quarters, mine = n_x * n_l, x * n_l + z_near
+        across, along = lax.rem(x + 1, n_x) * n_l + z_near, x * n_l + lax.rem(z_near + 1, n_l)
+        last = lax.rem(x + 1, n_x) * n_l + lax.rem(z_near + 1, n_l)
+
+        def spot(k, which, halves=1, half=0):
+            return rows_of(dst.at[CORES * k], which * halves + half, quarters * halves)
+
+        def pass_on(k, n):
+            which = (mine, across, along, last)[n]
+            there = rows_of(dst.at[CORES * k + 1], which, quarters)
+            copies.start((name, "core", k, n), spot(k, which), there, core)
+
+        far = range(1, n_y)
+        copies.start((name, "core", 0), src, dst.at[1], core)
+        for k in far:
+            copies.start(
+                (name, "y", k), rows_of(src, mine, quarters), spot(k, mine), t_peer(n_y - k, 0)
+            )
+        yield
+        for k in far:
+            copies.arrived((name, "y", k), spot(k, mine), core)
+            copies.start((name, "x", k), spot(k, mine), spot(k, mine), x_peer(1))
+            copies.start((name, "l", k), spot(k, mine), spot(k, mine), l_peer(1))
+            pass_on(k, 0)
+        yield
+        for k in far:
+            copies.arrived((name, "x", k), spot(k, across), core)
+            first = spot(k, across, 2, 0)
+            copies.start((name, "xl", k), first, first, l_peer(1))
+            copies.arrived((name, "l", k), spot(k, along), core)
+            second = spot(k, along, 2, 1)
+            copies.start((name, "lx", k), second, second, x_peer(1))
+            pass_on(k, 1)
+            pass_on(k, 2)
+        yield
+        for k in far:
+            copies.arrived((name, "xl", k), spot(k, last, 2, 0), core)
+            copies.arrived((name, "lx", k), spot(k, last, 2, 1), core)
+            pass_on(k, 3)
+        yield
+
+    def whole(name, s):
+        _, dst = full[name]
+        quarters = n_x * n_l
+        if s == 1:
+            copies.arrived((name, "core", 0), dst.at[1], core)
+        elif s % CORES == 1:
+            here, there = lax.rem(x + 1, n_x) * n_l, lax.rem(z_near + 1, n_l)
+            spots = [x * n_l + z_near, here + z_near, x * n_l + there, here + there]
+            for n, which in enumerate(spots):
+                got = rows_of(dst.at[s], which, quarters)
+                copies.arrived((name, "core", s // CORES, n), got, core)
+
+    position = {"x": x, "l": z_near, "h": z_far}
+    extent = {"x": n_x, "l": n_l, "h": n_h}
+    neighbour = {"x": x_peer, "l": l_peer, "h": h_peer}
+    reduced = {}
+
+    def take(ref, dims, axis, which):
+        return ref.at[(slice(None),) * dims.index(axis) + (which,)]
+
+    def spots_of(dims):
+        spots = [()]
+        for axis in dims:
+            spots = [spot + (a,) for spot in spots for a in range(extent[axis])]
+        return spots
+
+    def sum_f32(values):
+        return functools.reduce(lambda a, b: a + b, [v.astype(F32) for v in values])
+
+    def send_parts(name, cur, dims, axis, recv):
+        for j in range(1, extent[axis]):
+            which = lax.rem(position[axis] + j, extent[axis])
+            copies.start(
+                (name, axis, j), take(cur, dims, axis, which), recv.at[j - 1], neighbour[axis](j)
+            )
+
+    def fold(name, cur, dims, axis, recv, keep=True):
+        for j in range(1, extent[axis]):
+            copies.arrived((name, axis, j), recv.at[j - 1], core)
+        at_axis = dims.index(axis)
+        rest = [d for d in dims if d != axis]
+        total = None
+        for spot in spots_of(rest):
+            mine = cur[spot[:at_axis] + (position[axis],) + spot[at_axis:]]
+            total = sum_f32([mine] + [recv[(j,) + spot] for j in range(extent[axis] - 1)])
+            if keep:
+                recv[(0,) + spot] = total.astype(BF)
+        return (recv.at[0] if keep else total), rest
+
+    def reduce_pair(tag, bufs, k):
+        order = ORDER[tag]
+        own, got = bufs[:2]
+        copies.start((tag, "core", k), own.at[CORES * k + 1], got.at[k], core)
+        yield
+        copies.arrived((tag, "core", k), got.at[k], core)
+        for spot in spots_of(["h", "l", "x"]):
+            here = (CORES * k,) + spot
+            own[here] = own[here] + got[(k,) + spot]
+        cur, dims = own.at[CORES * k], ["h", "l", "x"]
+        for n, axis in enumerate(order[: order.index("y")]):
+            recv = bufs[2 + n].at[k]
+            send_parts((tag, k), cur, dims, axis, recv)
+            yield
+            cur, dims = fold((tag, k), cur, dims, axis, recv)
+        if k > 0:
+            copies.start((tag, "y", k), cur, bufs[2 + order.index("y")].at[k - 1], t_peer(k, 0))
+        reduced[tag, k] = cur, dims
+        yield
+
+    def reduce_end(tag, bufs, write):
+        order = ORDER[tag]
+        cur, dims = reduced[tag, 0]
+        at_y = order.index("y")
+        recv = bufs[2 + at_y]
+        for k in range(1, n_y):
+            copies.arrived((tag, "y", k), recv.at[k - 1], core)
+        total = None
+        for spot in spots_of(dims):
+            total = sum_f32([cur[spot]] + [recv[(k,) + spot] for k in range(n_y - 1)])
+            if dims:
+                recv[(0,) + spot] = total.astype(BF)
+        cur = recv.at[0]
+        for n, axis in enumerate(order[at_y + 1 :]):
+            recv = bufs[3 + at_y + n]
+            send_parts(tag, cur, dims, axis, recv)
+            yield
+            cur, dims = fold(tag, cur, dims, axis, recv, len(dims) > 1)
+            total = cur
+        write(total)
+        yield
+
+    def write_up(total):
+        gu_ref[...] = total
+
+    def write_down(total):
+        gd_ref[...] = total
+
+    def write_proj(total):
+        gp_ref[...] = total
+
+    def write_query_key(total):
+        gq_ref[0] = total[:, :heads_w]
+        gq_ref[1] = total[:, heads_w:]
+
+    def write_value(total):
+        gq_ref[2] = total
+
+    def vectors():
+        for s in range(n_t):
+            lines = [jnp.sum(vec_acc[k], axis=0, keepdims=True) for k in range(6)]
+            lines.append(jnp.sum(bup_acc[s], axis=0, keepdims=True))
+            lines.append(jnp.zeros((1, width), F32))
+            vec_mine[s] = jnp.concatenate(lines, axis=0)
+        for s in range(1, n_t):
+            copies.start(("vt", s), vec_mine.at[s], vec_t.at[s - 1], t_peer(s // CORES, s % CORES))
+        yield
+        total = vec_mine[0]
+        for s in range(1, n_t):
+            copies.arrived(("vt", s), vec_t.at[s - 1], core)
+            total = total + vec_t[s - 1]
+        vec_sum[...] = total
+        for k in range(1, n_dp):
+            copies.start(("vd", k), vec_sum, vec_dp.at[k - 1], (lax.rem(d + k, n_dp), t))
+        yield
+        for k in range(1, n_dp):
+            copies.arrived(("vd", k), vec_dp.at[k - 1], core)
+            total = total + vec_dp[k - 1]
+        gv_ref[...] = total
+        yield
+
+    u_own, d_own, p_own = u_bufs[0], d_bufs[0], p_bufs[0]
+    qk_own, v_own = qk_bufs[0], v_bufs[0]
+    sums = {
+        "u": (u_bufs, write_up),
+        "d": (d_bufs, write_down),
+        "p": (p_bufs, write_proj),
+        "qk": (qk_bufs, write_query_key),
+        "v": (v_bufs, write_value),
+    }
+    steps = {name: gather(name) for name in full}
+    for tag, (bufs, write) in sums.items():
+        for k in range(n_y):
+            steps[tag + str(k)] = reduce_pair(tag, bufs, k)
+        steps[tag] = reduce_end(tag, bufs, write)
+    steps["vec"] = vectors()
+
+    def tick(name):
+        for step in SCHEDULE.get(name, ()):
+            next(steps[step])
+
+    tick("start")
+    for s in range(1, n_t):
+        copies.start(
+            ("bu", s),
+            bu.at[0],
+            bu.at[s],
+            t_peer((n_y - s // CORES) % n_y, (CORES - s % CORES) % CORES),
+        )
 
     first_head = lax.broadcasted_iota(jnp.int32, (BLOCK, heads_w), 1) < HD
 
@@ -543,62 +729,67 @@
         own = jnp.concatenate([both[:HD, :BLOCK], both[HD:, BLOCK:]], axis=0)
         return own.T
 
-    def project_heads(s):
-        @pl.loop(0, rows // ROWS)
+    def qkv_weight(slots):
+        return jnp.concatenate([wq[s, j] for s in slots for j in range(3)], axis=1)
+
+    def project_heads(slots):
+        @pl.loop(0, rows // WIDE_ROWS)
         def _(i):
-            here = at(i, ROWS)
-            got = mm(n1[here, :], wq[s])
-            qs[s, here, :] = got[:, :heads_w].astype(BF) * jnp.asarray(HD**-0.5, BF)
-            k = got[:, heads_w : 2 * heads_w].astype(BF)
-            v = got[:, 2 * heads_w :].astype(BF)
-            there = at(i, ROWS, BLOCK)
-            ks[s, there, :] = k
-            vs[s, there, :] = v
-            ks_t[s, :, there] = k.T
-            vs_t[s, :, there] = v.T
+            here = at(i, WIDE_ROWS)
+            there = at(i, WIDE_ROWS, BLOCK)
+            all_of = mm(n1[here, :], qkv_weight(slots)).astype(BF)
+            for n, s in enumerate(slots):
+                got = all_of[:, n * qkv_w : (n + 1) * qkv_w]
+                qs[s, here, :] = got[:, :heads_w] * jnp.asarray(HD**-0.5, BF)
+                k = got[:, heads_w : 2 * heads_w]
+                v = got[:, 2 * heads_w :]
+                ks[s, there, :] = k
+                vs[s, there, :] = v
+                ks_t[s, :, there] = k.T
+                vs_t[s, :, there] = v.T
+
+    heres = [pl.ds(i * BLOCK, BLOCK) for i in range(blocks)]
+    seens = [pl.ds(i * BLOCK, 2 * BLOCK) for i in range(blocks)]
 
     def attend_slot(s):
-        @pl.loop(0, blocks)
-        def _(i):
-            here = at(i, BLOCK)
-            seen = pl.ds(pl.multiple_of(i * BLOCK, BLOCK), 2 * BLOCK)
+        scores = [
+            mm_nt(ks[s, seen, :], two_heads(qs[s, here, :])) for here, seen in zip(heres, seens)
+        ]
+        lows = []
+        for i in range(blocks):
             one = bias[i]
-            scores = mm_nt(ks[s, seen, :], two_heads(qs[s, here, :]))
-            scores = scores + jnp.concatenate([one, one], axis=1)
-            peak = jnp.max(scores, axis=0, keepdims=True)
-            expo = jnp.exp(scores - peak)
+            score = scores[i] + jnp.concatenate([one, one], axis=1)
+            expo = jnp.exp(score - jnp.max(score, axis=0, keepdims=True))
             total = jnp.sum(expo, axis=0, keepdims=True)
             low = (expo * (1.0 / total)).astype(BF)
             probs[s, i] = low
-            mixed[here, s * heads_w : (s + 1) * heads_w] = pick_heads(
-                mm(vs_t[s, :, seen], low)
-            ).astype(BF)
+            lows.append(low)
+        both = [mm(vs_t[s, :, seen], low) for seen, low in zip(seens, lows)]
+        for i in range(blocks):
+            mixed[heres[i], s * heads_w : (s + 1) * heads_w] = pick_heads(both[i]).astype(BF)
 
     load_wq.wait()
-    project_heads(0)
+    whole("wq", 1)
+    project_heads((0, 1))
+    tick("heads0")
     attend_slot(0)
-    gather_first("wq")
-    gather_send("wp")
-    gather_send("wu")
-    gather_wait("wq", 1)
-    project_heads(1)
+    tick("attend0")
     attend_slot(1)
-    gather_second("wq")
-    for s in range(2, n_t):
-        if s == 3:
-            gather_first("wp")
-            gather_first("wu")
-            gather_send("wd")
-        gather_wait("wq", s)
-        project_heads(s)
-        attend_slot(s)
-    gather_second("wp")
-    gather_second("wu")
+    tick("attend1")
+    for k in range(1, n_y):
+        slots = (CORES * k, CORES * k + 1)
+        whole("wq", slots[0])
+        whole("wq", slots[1])
+        project_heads(slots)
+        tick(f"heads{slots[0]}")
+        for s in slots:
+            attend_slot(s)
+            tick(f"attend{s}")
 
     load_wp.wait()
     load_dy.wait()
     for s in range(1, n_t):
-        gather_wait("wp", s)
+        whole("wp", s)
 
     @pl.loop(0, rows // ROWS)
     def _(i):
@@ -611,15 +802,14 @@
         r = lax.rsqrt(jnp.mean(centre * centre, axis=-1, keepdims=True) + epsilon)
         normed = (centre * r * ln2_gain + ln2_bias).astype(BF)
         n2[here, :] = normed
-        n2_t[:, here] = normed.T
         stats[2, here, :] = jnp.broadcast_to(mean, (ROWS, BLOCK))
         stats[3, here, :] = jnp.broadcast_to(r, (ROWS, BLOCK))
-        dy_t[:, here] = dy[here, :].T
-
-    def mlp_slot(s):
-        @pl.loop(0, rows // ROWS)
-        def _(i):
-            here = at(i, ROWS)
+
+    tick("hidden")
+
+    def mlp_slot(s, new):
+        for i in range(rows // WIDE_ROWS):
+            here = pl.ds(i * WIDE_ROWS, WIDE_ROWS)
             u = mm(n2[here, :], wu[s]) + bu[s, 0:1, :]
             dact = mm_nt(dy[here, :], wd[s])
             cdf, bell = normal_parts(u)
@@ -630,100 +820,30 @@
             bup_acc[s] += by_eight(du.astype(F32))
             up_part = mm(active, wd[s])
             back_part = mm_nt(du, wu[s])
-            if s == 0:
+            if new:
                 out_acc[here, :] = up_part
                 dn2_acc[here, :] = back_part
             else:
                 out_acc[here, :] += up_part
                 dn2_acc[here, :] += back_part
-
-        tile = 2 * n_x * m_own.shape[3]
-
-        @pl.loop(0, width // tile)
-        def _(j):
-            here = at(j, tile)
-            split = (2, n_x, m_own.shape[3], hidden_w)
-            m_own[s, pl.ds(2 * j, 2), :, :, 0:hidden_w] = (
-                mm(n2_t[here, :], dup[...]).astype(BF).reshape(split)
-            )
-            m_own[s, pl.ds(2 * j, 2), :, :, hidden_w:] = (
-                mm(dy_t[here, :], act[...]).astype(BF).reshape(split)
-            )
-
-    def rs_core_send(tag, own, got, k):
-        copies.start((tag, "c", k), own.at[CORES * k + 1], got.at[k], core)
-
-    def rs_x_send(tag, own, got, after, k):
-        copies.arrived((tag, "c", k), got.at[k], core)
-
-        @pl.loop(0, n_z)
-        def _(a):
-            own[CORES * k, a] = own[CORES * k, a] + got[k, a]
-
-        for j in range(1, n_x):
-            which = lax.rem(x + j, n_x)
-            copies.start(
-                (tag, "x", k, j), own.at[CORES * k, :, which], after.at[k, j - 1], x_peer(j)
-            )
-
-    def rs_x_sum(tag, own, after, k):
-        for j in range(1, n_x):
-            copies.arrived((tag, "x", k, j), after.at[k, j - 1], core)
-
-        @pl.loop(0, n_z)
-        def _(a):
-            total = own[CORES * k, a, x].astype(F32)
-            for j in range(1, n_x):
-                total = total + after[k, j - 1, a].astype(F32)
-            after[k, 0, a] = total.astype(BF)
-
-    def rs_y_send(tag, after, got, k):
-        copies.start((tag, "y", k), after.at[k, 0], got.at[k - 1], t_peer(k, 0))
-
-    def rs_z_send(tag, after, got, last):
-        for k in range(1, n_y):
-            copies.arrived((tag, "y", k), got.at[k - 1], core)
-
-        @pl.loop(0, n_z)
-        def _(a):
-            total = after[0, 0, a].astype(F32)
-            for k in range(1, n_y):
-                total = total + got[k - 1, a].astype(F32)
-            after[0, 0, a] = total.astype(BF)
-
-        for k in range(1, n_z):
-            copies.start(
-                (tag, "z", k), after.at[0, 0, lax.rem(z + k, n_z)], last.at[k - 1], z_peer(k)
-            )
-
-    def rs_finish(tag, after, last, result):
-        for k in range(1, n_z):
-            copies.arrived((tag, "z", k), last.at[k - 1], core)
-        total = after[0, 0, z].astype(F32)
-        for k in range(1, n_z):
-            total = total + last[k - 1].astype(F32)
-        result[...] = total
+            tick(f"rows{s}.{i}")
+        split = (n_h, n_l, n_x, part, hidden_w)
+        u_own[s] = mm_tn(n2[...], dup[...]).astype(BF).reshape(split)
+        d_own[s] = mm_tn(dy[...], act[...]).astype(BF).reshape(split)
+        tick(f"mlp{s}")
 
     load_wu.wait()
     load_wd.wait()
     for s in range(1, n_t):
         copies.arrived(("bu", s), bu.at[s], core)
-    gather_first("wd")
-    mlp_slot(0)
-    gather_second("wd")
-    for s in range(1, n_t):
-        gather_wait("wu", s)
-        gather_wait("wd", s)
-        mlp_slot(s)
-        if s % CORES == 1:
-            rs_core_send("m", m_own, m_core, s // CORES)
-        elif s >= 2:
-            rs_x_send("m", m_own, m_core, m_x, s // CORES - 1)
-    rs_x_send("m", m_own, m_core, m_x, n_y - 1)
-
-    @pl.loop(0, rows // ROWS)
-    def _(i):
-        here = at(i, ROWS)
+    order = [s + 1 - 2 * (s % CORES) for s in range(n_t)]
+    for s in order:
+        whole("wu", s)
+        whole("wd", s)
+        mlp_slot(s, s == order[0])
+
+    for i in range(rows // WIDE_ROWS):
+        here = pl.ds(i * WIDE_ROWS, WIDE_ROWS)
         value = hidden[here, :]
         out_b[here, :] = (value + out_acc[here, :] + down_bias).astype(BF)
         mean = stats[2, here, 0:1]
@@ -737,78 +857,53 @@
         dh = g + r * (scaled - first - xhat * second)
         hidden[here, :] = dh
         low = dh.astype(BF)
-        dy_t[:, here] = low.T
+        branch[here, :] = low
         dmixed[here, :] = mm_nt(low, wp[...].reshape(n_t * heads_w, width)).astype(BF)
         vec_acc[2] += by_eight(dh)
         vec_acc[3] += by_eight(dn * xhat)
         vec_acc[4] += by_eight(dn)
         vec_acc[5] += by_eight(g)
+        tick(f"norm2.{i}")
 
     store_out = local(out_b, out_h, 6)
 
-    qkv_w = 3 * heads_w
-    tile = 2 * n_x * q_own.shape[3]
-
-    @pl.loop(0, width // tile)
-    def _(j):
-        got = mm(dy_t[at(j, tile), :], mixed[...]).astype(BF)
-        for s in range(n_t):
-            q_own[s, pl.ds(2 * j, 2), :, :, qkv_w:] = got[
-                :, s * heads_w : (s + 1) * heads_w
-            ].reshape(2, n_x, q_own.shape[3], heads_w)
+    got = mm_tn(branch[...], mixed[...]).astype(BF)
+    for s in range(n_t):
+        p_own[s] = got[:, s * heads_w : (s + 1) * heads_w].reshape(n_h, n_l, n_x, part, heads_w)
+    tick("proj")
 
     def attend_back_slot(s):
-        carry[...] = jnp.zeros_like(carry)
-
-        @pl.loop(0, blocks)
-        def _(i):
-            here = at(i, BLOCK)
-            seen = pl.ds(pl.multiple_of(i * BLOCK, BLOCK), 2 * BLOCK)
-            grad = two_heads(dmixed[here, s * heads_w : (s + 1) * heads_w])
-            low = probs[s, i]
-            p = low.astype(F32)
-            weighed = p * mm_nt(vs[s, seen, :], grad)
-            ds = (weighed - p * jnp.sum(weighed, axis=0, keepdims=True)).astype(BF)
-            dv = mm(low, grad)
-            dk = mm(ds, two_heads(qs[s, here, :]))
-            dq = pick_heads(mm(ks_t[s, :, seen], ds)) * (HD**-0.5)
-            dtri[s, at(i, BLOCK, BLOCK), 0:heads_w] = dq.astype(BF)
-            dtri[s, here, heads_w : 2 * heads_w] = (carry[0] + dk[:BLOCK]).astype(BF)
-            dtri[s, here, 2 * heads_w :] = (carry[1] + dv[:BLOCK]).astype(BF)
-            carry[0] = dk[BLOCK:]
-            carry[1] = dv[BLOCK:]
-
-        dtri[s, rows:, heads_w : 2 * heads_w] = carry[0].astype(BF)
-        dtri[s, rows:, 2 * heads_w :] = carry[1].astype(BF)
-
-        @pl.loop(0, width // tile)
-        def _(j):
-            q_own[s, pl.ds(2 * j, 2), :, :, 0:qkv_w] = (
-                mm(n1_t[at(j, tile), :], dtri[s, BLOCK:, :])
-                .astype(BF)
-                .reshape(2, n_x, q_own.shape[3], qkv_w)
-            )
-
-    for k in reversed(range(n_y)):
-        attend_back_slot(CORES * k + 1)
-        rs_core_send("q", q_own, q_core, k)
-        rs_x_sum("m", m_own, m_x, k)
-        if k > 0:
-            rs_y_send("m", m_x, m_y, k)
-        if k < n_y - 1:
-            rs_x_sum("q", q_own, q_x, k + 1)
-            rs_y_send("q", q_x, q_y, k + 1)
-        attend_back_slot(CORES * k)
-        rs_x_send("q", q_own, q_core, q_x, k)
-    rs_z_send("m", m_x, m_y, m_z)
-
-    @pl.loop(0, rows // ROWS)
-    def _(i):
-        here = at(i, ROWS)
-        there = at(i, ROWS, BLOCK)
-        dn = mm_nt(dtri[0, there, :], wq[0])
-        for s in range(1, n_t):
-            dn = dn + mm_nt(dtri[s, there, :], wq[s])
+        lanes = slice(s * heads_w, (s + 1) * heads_w)
+        first = s * qkv_w
+        grads = [two_heads(dmixed[here, lanes]) for here in heres]
+        dprobs = [mm_nt(vs[s, seen, :], grad) for seen, grad in zip(seens, grads)]
+        ds = []
+        for i in range(blocks):
+            p = probs[s, i].astype(F32)
+            weighed = p * dprobs[i]
+            ds.append((weighed - p * jnp.sum(weighed, axis=0, keepdims=True)).astype(BF))
+        dv = [mm(probs[s, i], grads[i]) for i in range(blocks)]
+        dk = [mm(ds[i], two_heads(qs[s, heres[i], :])) for i in range(blocks)]
+        dq = [pick_heads(mm(ks_t[s, :, seens[i]], ds[i])) * (HD**-0.5) for i in range(blocks)]
+        for i in range(blocks):
+            k_sum, v_sum = dk[i][BLOCK:], dv[i][BLOCK:]
+            if i + 1 < blocks:
+                k_sum, v_sum = k_sum + dk[i + 1][:BLOCK], v_sum + dv[i + 1][:BLOCK]
+            dtri[heres[i], first : first + heads_w] = dq[i].astype(BF)
+            dtri[heres[i], first + heads_w : first + 2 * heads_w] = k_sum.astype(BF)
+            dtri[heres[i], first + 2 * heads_w : first + qkv_w] = v_sum.astype(BF)
+        tick(f"back{s}")
+        got = mm_tn(n1[...], dtri[:, first : first + qkv_w]).astype(BF)
+        qk_own[s] = got[:, : 2 * heads_w].reshape(n_h, n_l, n_x, part, 2 * heads_w)
+        v_own[s] = got[:, 2 * heads_w :].reshape(n_h, n_l, n_x, part, heads_w)
+        tick(f"qkv{s}")
+
+    for s in reversed(range(n_t)):
+        attend_back_slot(s)
+
+    for i in range(rows // WIDE_ROWS):
+        here = pl.ds(i * WIDE_ROWS, WIDE_ROWS)
+        dn = mm_nt(dtri[here, :], qkv_weight(range(n_t)))
         mean = stats[0, here, 0:1]
         r = stats[1, here, 0:1]
         xhat = (tok[here, :].astype(F32) - mean) * r
@@ -818,36 +913,35 @@
         gtok_b[here, :] = (hidden[here, :] + r * (scaled - first - xhat * second)).astype(BF)
         vec_acc[0] += by_eight(dn * xhat)
         vec_acc[1] += by_eight(dn)
+        tick(f"norm1.{i}")
 
     store_gtok = local(gtok_b, gtok_h, 7)
 
-    for s in range(n_t):
-        lines = [jnp.sum(vec_acc[k], axis=0, keepdims=True) for k in range(6)]
-        lines.append(jnp.sum(bup_acc[s], axis=0, keepdims=True))
-        lines.append(jnp.zeros((1, width), F32))
-        vec_mine[s] = jnp.concatenate(lines, axis=0)
-    for s in range(1, n_t):
-        copies.start(
-            ("vt", s), vec_mine.at[s], vec_t.at[s - 1], t_peer(s // CORES, s % CORES)
-        )
-    rs_x_sum("q", q_own, q_x, 0)
-    rs_z_send("q", q_x, q_y, q_z)
-    total = vec_mine[0]
-    for s in range(1, n_t):
-        copies.arrived(("vt", s), vec_t.at[s - 1], core)
-        total = total + vec_t[s - 1]
-    vec_sum[...] = total
-    for k in range(1, n_dp):
-        copies.start(("vd", k), vec_sum, vec_dp.at[k - 1], (lax.rem(d + k, n_dp), t))
-    rs_finish("m", m_x, m_z, gm_ref)
-    for k in range(1, n_dp):
-        copies.arrived(("vd", k), vec_dp.at[k - 1], core)
-        total = total + vec_dp[k - 1]
-    gv_ref[...] = total
-    rs_finish("q", q_x, q_z, gq_ref)
+    tick("end")
     store_out.wait()
     store_gtok.wait()
     copies.drain()
+
+
+def result_kernel(sizes, *refs):
+    n_t, n_dp, hidden_w = sizes
+    sources, vec, results, shares, sems = refs[:6], refs[6], refs[7:13], refs[13:20], refs[20]
+    copies = [
+        pltpu.make_async_copy(src, dst, sems.at[i])
+        for i, (src, dst) in enumerate(zip(sources, results))
+    ]
+    for copy in copies:
+        copy.start()
+    d, t = lax.axis_index("dp"), lax.axis_index("tensor")
+    width = vec.shape[1]
+    first = (d * n_t + t) * (width // (n_dp * n_t))
+    lines = pltpu.roll(vec[...], lax.rem(width - first, width), 1)
+    for i in range(6):
+        shares[i][...] = lines[i : i + 1, : shares[i].shape[1]]
+    lines = pltpu.roll(vec[...], lax.rem(width - d * (hidden_w // n_dp), width), 1)
+    shares[6][...] = lines[6:7, : shares[6].shape[1]]
+    for copy in copies:
+        copy.wait()
 
 
 def fused_device(
@@ -871,22 +965,26 @@
     _, rows, width = tokens.shape
     heads_w = projection_weight.shape[0]
     hidden_w = up_weight.shape[1]
-    n_y, n_x, n_z = n_t // CORES, WIDE, n_dp // WIDE
+    n_y, n_x, n_l, n_h = n_t // CORES, WIDE, PAIR, n_dp // (WIDE * PAIR)
     part = width // n_dp
     blocks = rows // BLOCK
     qkv_w = 3 * heads_w
-    vecs = jnp.stack(
-        [ln1_gain, ln1_bias, attention_output_bias, ln2_gain, ln2_bias, mlp_down_bias]
-    )
-
-    def chunk(w):
-        return [
-            pltpu.VMEM((n_t, n_z, n_x, part, w), BF),
-            pltpu.VMEM((n_y, n_z, n_x, part, w), BF),
-            pltpu.VMEM((n_y, n_x - 1, n_z, part, w), BF),
-            pltpu.VMEM((n_y - 1, n_z, part, w), BF),
-            pltpu.VMEM((n_z - 1, part, w), BF),
+    def chunk(tag, w):
+        sizes = {"h": n_h, "l": n_l, "x": n_x}
+        dims, early = ["h", "l", "x"], True
+        bufs = [
+            pltpu.VMEM((n_t, n_h, n_l, n_x, part, w), BF),
+            pltpu.VMEM((n_y, n_h, n_l, n_x, part, w), BF),
         ]
+        for axis in ORDER[tag]:
+            if axis == "y":
+                early = False
+                lead = (n_y - 1,)
+            else:
+                dims = [a for a in dims if a != axis]
+                lead = ((n_y,) if early else ()) + (sizes[axis] - 1,)
+            bufs.append(pltpu.VMEM(lead + tuple(sizes[a] for a in dims) + (part, w), BF))
+        return bufs
 
     def half(*shape):
         return pltpu.VMEM(shape, BF)
@@ -897,14 +995,12 @@
     scratch = [
         half(rows, width),
         half(rows, width),
-        half(width, rows),
-        half(n_t, width, qkv_w),
+        half(n_t, 3, width, heads_w),
         half(n_t, heads_w, width),
         half(n_t, width, hidden_w),
         half(n_t, hidden_w, width),
         single(n_t, 8, hidden_w),
         half(rows, width),
-        half(width, rows),
         single(4, rows, BLOCK),
         half(n_t, rows, heads_w),
         half(n_t, rows + BLOCK, heads_w),
@@ -916,41 +1012,45 @@
         half(rows, n_t * heads_w),
         single(rows, width),
         half(rows, width),
-        half(width, rows),
         single(rows, width),
         single(rows, width),
         half(rows, hidden_w),
         half(rows, hidden_w),
+        half(rows, width),
         half(rows, n_t * heads_w),
-        half(n_t, rows + BLOCK, qkv_w),
-        single(2, BLOCK, heads_w),
+        half(rows, n_t * qkv_w),
         single(6, 8, width),
         single(n_t, 8, hidden_w),
         single(n_t, 8, width),
         single(n_t - 1, 8, width),
         single(8, width),
         single(n_dp - 1, 8, width),
-        *chunk(2 * hidden_w),
-        *chunk(qkv_w + heads_w),
+        chunk("u", hidden_w),
+        chunk("d", hidden_w),
+        chunk("p", heads_w),
+        chunk("qk", 2 * heads_w),
+        chunk("v", heads_w),
         half(rows, width),
         half(rows, width),
         pltpu.SemaphoreType.DMA((8,)),
-        pltpu.SemaphoreType.DMA((64,)),
-        pltpu.SemaphoreType.DMA((64,)),
+        pltpu.SemaphoreType.DMA((128,)),
+        pltpu.SemaphoreType.DMA((128,)),
     ]
     anywhere = pl.BlockSpec(memory_space=pl.ANY)
     near = pl.BlockSpec(memory_space=pltpu.VMEM)
-    out, gtok, gm, gq, gv = pl.pallas_call(
+    results = pl.pallas_call(
         functools.partial(layer_kernel, (n_t, n_dp, rows, width, heads_w, hidden_w)),
         out_shape=(
             jax.ShapeDtypeStruct((rows, width), BF),
             jax.ShapeDtypeStruct((rows, width), BF),
-            jax.ShapeDtypeStruct((part, 2 * hidden_w), F32),
-            jax.ShapeDtypeStruct((part, qkv_w + heads_w), F32),
+            jax.ShapeDtypeStruct((3, part, heads_w), F32),
+            jax.ShapeDtypeStruct((part, heads_w), F32),
+            jax.ShapeDtypeStruct((part, hidden_w), F32),
+            jax.ShapeDtypeStruct((part, hidden_w), F32),
             jax.ShapeDtypeStruct((8, width), F32),
         ),
-        in_specs=[anywhere, anywhere, near, near, near] + [anywhere] * 4,
-        out_specs=(anywhere, anywhere, near, near, near),
+        in_specs=[anywhere] * 2 + [near] * 8 + [anywhere] * 4,
+        out_specs=[anywhere] * 2 + [near] * 5,
         scratch_shapes=scratch,
         compiler_params=pltpu.CompilerParams(
             collective_id=0, has_side_effects=True, vmem_limit_bytes=63 << 20
@@ -959,30 +1059,42 @@
         tokens.reshape(rows, width),
         grad_output.reshape(rows, width),
         clip_ids,
-        vecs,
+        ln1_gain.reshape(1, width),
+        ln1_bias.reshape(1, width),
+        attention_output_bias.reshape(1, width),
+        ln2_gain.reshape(1, width),
+        ln2_bias.reshape(1, width),
+        mlp_down_bias.reshape(1, width),
         mlp_up_bias.reshape(1, hidden_w),
-        query_key_value_weight.reshape(width, qkv_w),
+        jnp.transpose(query_key_value_weight, (1, 0, 2)),
         projection_weight,
         up_weight,
         down_weight,
     )
-    d, t = lax.axis_index("dp"), lax.axis_index("tensor")
     share = width // (n_dp * n_t)
-    vectors = lax.dynamic_slice(gv, (0, (d * n_t + t) * share), (6, share))
-    g_up_bias = lax.dynamic_slice(gv, (6, d * (hidden_w // n_dp)), (1, hidden_w // n_dp))
+    out, gtok, gq, gp, gu, gd, *vectors, g_up_bias = pl.pallas_call(
+        functools.partial(result_kernel, (n_t, n_dp, hidden_w)),
+        out_shape=[jax.ShapeDtypeStruct(r.shape, r.dtype) for r in results[:6]]
+        + [jax.ShapeDtypeStruct((1, share), F32)] * 6
+        + [jax.ShapeDtypeStruct((1, hidden_w // n_dp), F32)],
+        in_specs=[near] * 7,
+        out_specs=[anywhere] * 6 + [near] * 7,
+        scratch_shapes=[pltpu.SemaphoreType.DMA((6,))],
+    )(*results)
+    vectors = [v.reshape(share) for v in vectors]
     return (
         out[None],
         gtok[None],
         vectors[0],
         vectors[1],
-        gq[:, :qkv_w].reshape(part, 3, heads_w),
-        gq[:, qkv_w:].T,
+        jnp.transpose(gq, (1, 0, 2)),
+        gp.T,
         vectors[2],
         vectors[3],
         vectors[4],
-        gm[:, :hidden_w],
+        gu,
         g_up_bias,
-        gm[:, hidden_w:].T,
+        gd.T,
         vectors[5],
     )
 

time: 131 us -> 86.3 us (0.66)
  Pallas kernels: 117 us -> 85.2 us
  local copies, waits for them, and re-layouts: 12.3 us -> 0 us
    pallas_call x1, Pallas kernels: 117 us -> 81.6 us  [fused_device(): pl.pallas_call(functools.partial(layer_kernel, (n_t, n_dp, rows, width, h...]
    unnamed x20 -> x0, local copies, waits for them, and re-layouts: 5.83 us -> none
    pallas_call x0 -> x1, Pallas kernels: none -> 3.67 us  [fused_device(): pl.pallas_call(functools.partial(result_kernel, (n_t, n_dp, hidden_w)), o...]
    transpose x2 -> x0, local copies, waits for them, and re-layouts: 2.34 us -> none  [the longest x1 1.72 us: fused_device(): gm[:, hidden_w:]]
    dynamic_slice x2 -> x0, local copies, waits for them, and re-layouts: 2 us -> none  [the longest x1 1.25 us: fused_device(): lax.dynamic_slice(gv, (6, d * (hidden_w // n_dp)), (1, hidden_w // n_dp))]
where the time goes in v2:
time: 86.3 us; the launch traced here: 86.1 us
  Pallas kernels  85.2 us (99%)
    pallas_call x1, Pallas kernels, fused_device(): pl.pallas_call(functools.partial(layer_kernel, (n_t, n_dp, rows, width, h...  81.6 us
    pallas_call x1, Pallas kernels, fused_device(): pl.pallas_call(functools.partial(result_kernel, (n_t, n_dp, hidden_w)), o...  3.67 us

profile of v2, /device:TPU:0, one launch (start us, length us, event | category | flops | bytes accessed | tf_op | source)
XLA Modules:
  0.0 86.1 jit_solution(17925309554885502396)
XLA Ops:
  0.7 81.6 %shard_map.237 = (bf16[1024,512]{1,0:T(8,128)(2,1)}, bf16[1024,512]{1,0:T(8,128)(2,1)}, f32[3,64,128]{2,1,0:T(8,128)}, f32[64,128]{1,0:T(8,128)}, f32[64,512]{1,...) custom-call(bf16[1024,512]{1,0:T(8,128)(2,1)} %bitcast.21, bf16[1024,512]{1,0:T(8,128)(2,1)} %bitcast.22, ...), custom_call_target="tpu_custom_call" | custom-call | tf_op jit(solution)/shard_map/pallas_call | solution.py:1041
  82.2 3.7 %shard_map.238 = (bf16[1024,512]{1,0:T(8,128)(2,1)}, bf16[1024,512]{1,0:T(8,128)(2,1)}, f32[3,64,128]{2,1,0:T(8,128)}, f32[64,128]{1,0:T(8,128)}, f32[64,512]{1,...) custom-call(bf16[1024,512]{1,0:T(8,128)(2,1)} %get-tuple-element.33., ...), custom_call_target="tpu_custom_call" | custom-call | tf_op jit(solution)/shard_map/pallas_call | solution.py:1075

commit v3 on v2

--- a/solution.py
+++ b/solution.py
@@ -274,33 +274,35 @@
 BLOCK = 128
 ROWS = 256
 WIDE_ROWS = 512
-
-ORDER = {"u": "xylh", "d": "lxyh", "p": "xylh", "qk": "xylh", "v": "lyxh"}
+PARTS = 4
+AXES = {"x": ("x",), "l": ("l",), "h": ("h",), "w": ("l", "x"), "z": ("h", "l")}
+SOON = ("wq",)
+
+ORDER = {"u": "xlg", "d": "lxg", "qk": "xlg", "pv": "ywh"}
 SCHEDULE = {
-    "start": ("wq", "wp",),
-    "heads0": ("wq",),
-    "attend0": ("wp", "wd", "wq", "wu",),
-    "attend1": ("wq", "wp",),
-    "heads2": ("wd",),
-    "attend2": ("wp",),
+    "start": ("wp", "wq", "wu", "wd",),
+    "heads0": ("wp",),
+    "attend0": ("wq",),
+    "attend1": ("wp", "wq", "wq",),
+    "dact": ("wp", "wu",),
+    "attend2": ("wd",),
     "hidden": ("wu",),
-    "mlp1": ("wd",),
-    "rows0.0": ("wu", "d0",),
-    "rows0.1": ("u0", "wd",),
-    "mlp0": ("wu", "d0", "u0",),
-    "rows2.1": ("d1", "d0", "u0", "u1",),
-    "mlp2": ("u1", "d1",),
-    "proj": ("p1",),
-    "back3": ("p0", "p1", "d0",),
-    "qkv3": ("qk1", "p0", "u1",),
-    "back2": ("d1",),
-    "qkv2": ("qk1",),
-    "back1": ("v1", "p1", "p0",),
-    "qkv1": ("qk0", "v1", "v0", "d1",),
-    "back0": ("p", "qk1", "u", "v1",),
-    "qkv0": ("qk0", "v0", "p", "d",),
-    "norm1.1": ("vec", "qk0", "qk", "u", "v0", "v", "v", "p",),
-    "end": ("vec", "qk", "v", "u", "d", "vec", "qk",),
+    "rows1.1": ("wd",),
+    "mlp1": ("d0",),
+    "rows0.0": ("wu", "u0",),
+    "rows0.1": ("wd",),
+    "mlp0": ("u0", "d0",),
+    "mlp3": ("u1", "d1",),
+    "mlp2": ("d1", "u1", "u0",),
+    "qkv3": ("d0", "qk1", "pv1",),
+    "qkv2": ("qk1", "u1", "pv1",),
+    "qkv1": ("u0", "d0", "qk0", "d1",),
+    "qkv0": ("qk1", "u1", "pv0", "qk0",),
+    "norm1.0": ("pv0", "pv",),
+    "norm1.1": ("vec", "d1",),
+    "out.0": ("qk0", "qk1", "u", "vec", "pv",),
+    "out.1": ("qk0", "vec",),
+    "end": ("d", "pv", "qk",),
 }
 
 
@@ -396,9 +398,9 @@
     mixed,
     hidden,
     n2,
-    out_acc,
     dn2_acc,
     act,
+    dact,
     dup,
     branch,
     dmixed,
@@ -411,9 +413,8 @@
     vec_dp,
     u_bufs,
     d_bufs,
-    p_bufs,
     qk_bufs,
-    v_bufs,
+    pv_bufs,
     out_b,
     gtok_b,
     local_sem,
@@ -436,14 +437,18 @@
     def x_peer(k):
         return (z * WIDE + lax.rem(x + k, n_x), t)
 
+    def dp_peer(h_off, l_off, x_off):
+        far, near = lax.rem(z_far + h_off, n_h), lax.rem(z_near + l_off, n_l)
+        return ((far * n_l + near) * WIDE + lax.rem(x + x_off, n_x), t)
+
     def l_peer(k):
-        return ((z_far * n_l + lax.rem(z_near + k, n_l)) * WIDE + x, t)
-
-    def h_peer(k):
-        return ((lax.rem(z_far + k, n_h) * n_l + z_near) * WIDE + x, t)
+        return dp_peer(0, k, 0)
 
     peers = [t_peer(s // CORES, s % CORES) for s in range(1, n_t)]
     peers += [(lax.rem(d + k, n_dp), t) for k in range(1, n_dp)]
+    for k in range(1, n_y):
+        for h in range(1, n_h):
+            peers.append((dp_peer(h, 0, 0)[0], t_peer(k, 0)[1]))
     core = t_peer(0, 1)
 
     barrier = pltpu.get_barrier_semaphore()
@@ -558,11 +563,55 @@
             pass_on(k, 3)
         yield
 
+    def gather_soon(name):
+        src, dst = full[name]
+        parts = 2 * n_x
+        far = range(1, n_y)
+
+        def spot(k, which, whole_half=False):
+            if whole_half:
+                return rows_of(dst.at[k], 1, 2)
+            return rows_of(dst.at[k], which, parts)
+
+        copies.start((name, "core", 0), src, dst.at[1], core)
+        for k in far:
+            peer = t_peer(n_y - k, 0)
+            copies.start((name, "y", k), rows_of(src, x, parts), spot(CORES * k, x), peer)
+        for k in far:
+            peer = t_peer(n_y - k, 0)
+            second = spot(CORES * k, 0, True)
+            copies.start((name, "yy", k), rows_of(src, 1, 2), second, peer)
+        yield
+        for k in far:
+            got = spot(CORES * k, x)
+            copies.arrived((name, "y", k), got, core)
+            for j in range(1, n_x):
+                copies.start((name, "x", k, j), got, got, x_peer(j))
+            copies.start((name, "core", k, 0), got, spot(CORES * k + 1, x), core)
+        yield
+        for k in far:
+            got = spot(CORES * k, 0, True)
+            copies.arrived((name, "yy", k), got, core)
+            copies.start((name, "core", k, n_x), got, spot(CORES * k + 1, 0, True), core)
+        yield
+        for k in far:
+            for j in range(1, n_x):
+                which = lax.rem(x + n_x - j, n_x)
+                got = spot(CORES * k, which)
+                copies.arrived((name, "x", k, j), got, core)
+                copies.start((name, "core", k, j), got, spot(CORES * k + 1, which), core)
+        yield
+
     def whole(name, s):
         _, dst = full[name]
         quarters = n_x * n_l
         if s == 1:
             copies.arrived((name, "core", 0), dst.at[1], core)
+        elif s % CORES == 1 and name in SOON:
+            for j in range(n_x):
+                got = rows_of(dst.at[s], lax.rem(x + n_x - j, n_x), 2 * n_x)
+                copies.arrived((name, "core", s // CORES, j), got, core)
+            copies.arrived((name, "core", s // CORES, n_x), rows_of(dst.at[s], 1, 2), core)
         elif s % CORES == 1:
             here, there = lax.rem(x + 1, n_x) * n_l, lax.rem(z_near + 1, n_l)
             spots = [x * n_l + z_near, here + z_near, x * n_l + there, here + there]
@@ -572,11 +621,18 @@
 
     position = {"x": x, "l": z_near, "h": z_far}
     extent = {"x": n_x, "l": n_l, "h": n_h}
-    neighbour = {"x": x_peer, "l": l_peer, "h": h_peer}
     reduced = {}
 
-    def take(ref, dims, axis, which):
-        return ref.at[(slice(None),) * dims.index(axis) + (which,)]
+    def steps_along(group):
+        offsets = [{}]
+        for axis in group:
+            offsets = [dict(o, **{axis: k}) for o in offsets for k in range(extent[axis])]
+        return [o for o in offsets if any(o.values())]
+
+    def part_for(dims, group, offset):
+        return tuple(
+            lax.rem(position[a] + offset[a], extent[a]) if a in group else slice(None) for a in dims
+        )
 
     def spots_of(dims):
         spots = [()]
@@ -587,28 +643,32 @@
     def sum_f32(values):
         return functools.reduce(lambda a, b: a + b, [v.astype(F32) for v in values])
 
-    def send_parts(name, cur, dims, axis, recv):
-        for j in range(1, extent[axis]):
-            which = lax.rem(position[axis] + j, extent[axis])
+    def send_parts(name, cur, dims, step, recv):
+        group = AXES[step]
+        for j, offset in enumerate(steps_along(group)):
+            peer = dp_peer(*(offset.get(a, 0) for a in ("h", "l", "x")))
             copies.start(
-                (name, axis, j), take(cur, dims, axis, which), recv.at[j - 1], neighbour[axis](j)
+                (name, step, j), cur.at[part_for(dims, group, offset)], recv.at[j], peer
             )
 
-    def fold(name, cur, dims, axis, recv, keep=True):
-        for j in range(1, extent[axis]):
-            copies.arrived((name, axis, j), recv.at[j - 1], core)
-        at_axis = dims.index(axis)
-        rest = [d for d in dims if d != axis]
+    def fold(name, cur, dims, step, recv, keep=True):
+        group = AXES[step]
+        others = len(steps_along(group))
+        for j in range(others):
+            copies.arrived((name, step, j), recv.at[j], core)
+        rest = [a for a in dims if a not in group]
         total = None
         for spot in spots_of(rest):
-            mine = cur[spot[:at_axis] + (position[axis],) + spot[at_axis:]]
-            total = sum_f32([mine] + [recv[(j,) + spot] for j in range(extent[axis] - 1)])
+            at_rest = dict(zip(rest, spot))
+            mine = cur[tuple(position[a] if a in group else at_rest[a] for a in dims)]
+            total = sum_f32([mine] + [recv[(j,) + spot] for j in range(others)])
             if keep:
                 recv[(0,) + spot] = total.astype(BF)
         return (recv.at[0] if keep else total), rest
 
     def reduce_pair(tag, bufs, k):
         order = ORDER[tag]
+        at_y = max(order.find("y"), order.find("g"))
         own, got = bufs[:2]
         copies.start((tag, "core", k), own.at[CORES * k + 1], got.at[k], core)
         yield
@@ -617,20 +677,37 @@
             here = (CORES * k,) + spot
             own[here] = own[here] + got[(k,) + spot]
         cur, dims = own.at[CORES * k], ["h", "l", "x"]
-        for n, axis in enumerate(order[: order.index("y")]):
+        for n, step in enumerate(order[: at_y]):
             recv = bufs[2 + n].at[k]
-            send_parts((tag, k), cur, dims, axis, recv)
+            send_parts((tag, k), cur, dims, step, recv)
             yield
-            cur, dims = fold((tag, k), cur, dims, axis, recv)
-        if k > 0:
-            copies.start((tag, "y", k), cur, bufs[2 + order.index("y")].at[k - 1], t_peer(k, 0))
+            cur, dims = fold((tag, k), cur, dims, step, recv)
+        if order[at_y] == "g":
+            recv = bufs[-1]
+            for off in range(n_h):
+                if k or off:
+                    mine = cur.at[part_for(dims, ("h",), {"h": off})]
+                    peer = (dp_peer(off, 0, 0)[0], t_peer(k, 0)[1])
+                    copies.start((tag, "g", k, off), mine, recv.at[k, off], peer)
+        elif k > 0:
+            copies.start((tag, "y", k), cur, bufs[2 + at_y].at[k - 1], t_peer(k, 0))
         reduced[tag, k] = cur, dims
         yield
 
     def reduce_end(tag, bufs, write):
         order = ORDER[tag]
         cur, dims = reduced[tag, 0]
-        at_y = order.index("y")
+        at_y = order.find("y")
+        if at_y < 0:
+            terms = [cur[z_far]]
+            for k in range(n_y):
+                for off in range(n_h):
+                    if k or off:
+                        copies.arrived((tag, "g", k, off), bufs[-1].at[k, off], core)
+                        terms.append(bufs[-1][k, off])
+            write(sum_f32(terms))
+            yield
+            return
         recv = bufs[2 + at_y]
         for k in range(1, n_y):
             copies.arrived((tag, "y", k), recv.at[k - 1], core)
@@ -640,11 +717,11 @@
             if dims:
                 recv[(0,) + spot] = total.astype(BF)
         cur = recv.at[0]
-        for n, axis in enumerate(order[at_y + 1 :]):
+        for n, step in enumerate(order[at_y + 1 :]):
             recv = bufs[3 + at_y + n]
-            send_parts(tag, cur, dims, axis, recv)
+            send_parts(tag, cur, dims, step, recv)
             yield
-            cur, dims = fold(tag, cur, dims, axis, recv, len(dims) > 1)
+            cur, dims = fold(tag, cur, dims, step, recv, at_y + 2 + n < len(order))
             total = cur
         write(total)
         yield
@@ -654,16 +731,17 @@
 
     def write_down(total):
         gd_ref[...] = total
-
-    def write_proj(total):
-        gp_ref[...] = total
 
     def write_query_key(total):
         gq_ref[0] = total[:, :heads_w]
         gq_ref[1] = total[:, heads_w:]
 
-    def write_value(total):
-        gq_ref[2] = total
+    def write_proj_value(total):
+        gp_ref[...] = total[:, :heads_w]
+        gq_ref[2] = total[:, heads_w:]
+
+    def lanes_of(who):
+        return pl.ds(pl.multiple_of(who * (width // n_dp) // BLOCK * BLOCK, BLOCK), BLOCK)
 
     def vectors():
         for s in range(n_t):
@@ -680,24 +758,24 @@
             total = total + vec_t[s - 1]
         vec_sum[...] = total
         for k in range(1, n_dp):
-            copies.start(("vd", k), vec_sum, vec_dp.at[k - 1], (lax.rem(d + k, n_dp), t))
-        yield
+            peer = lax.rem(d + k, n_dp)
+            copies.start(("vd", k), vec_sum.at[:, lanes_of(peer)], vec_dp.at[k - 1], (peer, t))
+        yield
+        total = vec_sum[:, lanes_of(d)]
         for k in range(1, n_dp):
             copies.arrived(("vd", k), vec_dp.at[k - 1], core)
             total = total + vec_dp[k - 1]
         gv_ref[...] = total
         yield
 
-    u_own, d_own, p_own = u_bufs[0], d_bufs[0], p_bufs[0]
-    qk_own, v_own = qk_bufs[0], v_bufs[0]
+    u_own, d_own, qk_own, pv_own = u_bufs[0], d_bufs[0], qk_bufs[0], pv_bufs[0]
     sums = {
         "u": (u_bufs, write_up),
         "d": (d_bufs, write_down),
-        "p": (p_bufs, write_proj),
         "qk": (qk_bufs, write_query_key),
-        "v": (v_bufs, write_value),
+        "pv": (pv_bufs, write_proj_value),
     }
-    steps = {name: gather(name) for name in full}
+    steps = {name: gather_soon(name) if name in SOON else gather(name) for name in full}
     for tag, (bufs, write) in sums.items():
         for k in range(n_y):
             steps[tag + str(k)] = reduce_pair(tag, bufs, k)
@@ -776,6 +854,12 @@
     tick("attend0")
     attend_slot(1)
     tick("attend1")
+    load_dy.wait()
+    load_wd.wait()
+    dact[0] = mm_nt(dy[...], wd[0]).astype(BF)
+    whole("wd", 1)
+    dact[1] = mm_nt(dy[...], wd[1]).astype(BF)
+    tick("dact")
     for k in range(1, n_y):
         slots = (CORES * k, CORES * k + 1)
         whole("wq", slots[0])
@@ -787,7 +871,6 @@
             tick(f"attend{s}")
 
     load_wp.wait()
-    load_dy.wait()
     for s in range(1, n_t):
         whole("wp", s)
 
@@ -808,44 +891,40 @@
     tick("hidden")
 
     def mlp_slot(s, new):
+        lanes = slice(s * hidden_w, (s + 1) * hidden_w)
         for i in range(rows // WIDE_ROWS):
             here = pl.ds(i * WIDE_ROWS, WIDE_ROWS)
             u = mm(n2[here, :], wu[s]) + bu[s, 0:1, :]
-            dact = mm_nt(dy[here, :], wd[s])
+            back = dact[s, here, :] if s < CORES else mm_nt(dy[here, :], wd[s])
             cdf, bell = normal_parts(u)
-            active = (u * cdf).astype(BF)
-            du = (dact * (cdf + bell)).astype(BF)
-            act[here, :] = active
+            act[here, lanes] = (u * cdf).astype(BF)
+            du = (back * (cdf + bell)).astype(BF)
             dup[here, :] = du
             bup_acc[s] += by_eight(du.astype(F32))
-            up_part = mm(active, wd[s])
             back_part = mm_nt(du, wu[s])
             if new:
-                out_acc[here, :] = up_part
                 dn2_acc[here, :] = back_part
             else:
-                out_acc[here, :] += up_part
                 dn2_acc[here, :] += back_part
             tick(f"rows{s}.{i}")
         split = (n_h, n_l, n_x, part, hidden_w)
         u_own[s] = mm_tn(n2[...], dup[...]).astype(BF).reshape(split)
-        d_own[s] = mm_tn(dy[...], act[...]).astype(BF).reshape(split)
+        d_own[s] = mm_tn(dy[...], act[:, lanes]).astype(BF).reshape(split)
         tick(f"mlp{s}")
 
     load_wu.wait()
-    load_wd.wait()
     for s in range(1, n_t):
         copies.arrived(("bu", s), bu.at[s], core)
     order = [s + 1 - 2 * (s % CORES) for s in range(n_t)]
     for s in order:
         whole("wu", s)
-        whole("wd", s)
+        if s != 1:
+            whole("wd", s)
         mlp_slot(s, s == order[0])
 
     for i in range(rows // WIDE_ROWS):
         here = pl.ds(i * WIDE_ROWS, WIDE_ROWS)
         value = hidden[here, :]
-        out_b[here, :] = (value + out_acc[here, :] + down_bias).astype(BF)
         mean = stats[2, here, 0:1]
         r = stats[3, here, 0:1]
         xhat = (value - mean) * r
@@ -855,7 +934,7 @@
         first = jnp.mean(scaled, axis=-1, keepdims=True)
         second = jnp.mean(scaled * xhat, axis=-1, keepdims=True)
         dh = g + r * (scaled - first - xhat * second)
-        hidden[here, :] = dh
+        dn2_acc[here, :] = dh
         low = dh.astype(BF)
         branch[here, :] = low
         dmixed[here, :] = mm_nt(low, wp[...].reshape(n_t * heads_w, width)).astype(BF)
@@ -865,11 +944,11 @@
         vec_acc[5] += by_eight(g)
         tick(f"norm2.{i}")
 
-    store_out = local(out_b, out_h, 6)
-
     got = mm_tn(branch[...], mixed[...]).astype(BF)
     for s in range(n_t):
-        p_own[s] = got[:, s * heads_w : (s + 1) * heads_w].reshape(n_h, n_l, n_x, part, heads_w)
+        pv_own[s, :, :, :, :, :heads_w] = got[:, s * heads_w : (s + 1) * heads_w].reshape(
+            n_h, n_l, n_x, part, heads_w
+        )
     tick("proj")
 
     def attend_back_slot(s):
@@ -895,7 +974,9 @@
         tick(f"back{s}")
         got = mm_tn(n1[...], dtri[:, first : first + qkv_w]).astype(BF)
         qk_own[s] = got[:, : 2 * heads_w].reshape(n_h, n_l, n_x, part, 2 * heads_w)
-        v_own[s] = got[:, 2 * heads_w :].reshape(n_h, n_l, n_x, part, heads_w)
+        pv_own[s, :, :, :, :, heads_w:] = got[:, 2 * heads_w :].reshape(
+            n_h, n_l, n_x, part, heads_w
+        )
         tick(f"qkv{s}")
 
     for s in reversed(range(n_t)):
@@ -910,12 +991,20 @@
         scaled = dn * ln1_gain
         first = jnp.mean(scaled, axis=-1, keepdims=True)
         second = jnp.mean(scaled * xhat, axis=-1, keepdims=True)
-        gtok_b[here, :] = (hidden[here, :] + r * (scaled - first - xhat * second)).astype(BF)
+        gtok_b[here, :] = (dn2_acc[here, :] + r * (scaled - first - xhat * second)).astype(BF)
         vec_acc[0] += by_eight(dn * xhat)
         vec_acc[1] += by_eight(dn)
         tick(f"norm1.{i}")
 
     store_gtok = local(gtok_b, gtok_h, 7)
+
+    for i in range(rows // WIDE_ROWS):
+        here = pl.ds(i * WIDE_ROWS, WIDE_ROWS)
+        grown = mm(act[here, :], wd[...].reshape(n_t * hidden_w, width))
+        out_b[here, :] = (hidden[here, :] + grown + down_bias).astype(BF)
+        tick(f"out.{i}")
+
+    store_out = local(out_b, out_h, 6)
 
     tick("end")
     store_out.wait()
@@ -924,24 +1013,32 @@
 
 
 def result_kernel(sizes, *refs):
-    n_t, n_dp, hidden_w = sizes
-    sources, vec, results, shares, sems = refs[:6], refs[6], refs[7:13], refs[13:20], refs[20]
-    copies = [
-        pltpu.make_async_copy(src, dst, sems.at[i])
-        for i, (src, dst) in enumerate(zip(sources, results))
-    ]
-    for copy in copies:
-        copy.start()
+    n_t, n_dp, width = sizes
+    sources, vec, results, shares = refs[:6], refs[6], refs[7:13], refs[13:20]
+    near, in_sems, out_sems = refs[20:26], refs[26], refs[27]
+    pieces = []
+    for src, mid, dst in zip(sources, near, results):
+        parts = PARTS if src.shape[0] % (PARTS * ROWS) == 0 else 1
+        step = src.shape[0] // parts
+        for i in range(parts):
+            here, at = pl.ds(i * step, step), len(pieces)
+            coming = pltpu.make_async_copy(src.at[here], mid.at[here], in_sems.at[at])
+            going = pltpu.make_async_copy(mid.at[here], dst.at[here], out_sems.at[at])
+            coming.start()
+            pieces.append((coming, going))
+    for coming, going in pieces:
+        coming.wait()
+        going.start()
     d, t = lax.axis_index("dp"), lax.axis_index("tensor")
-    width = vec.shape[1]
-    first = (d * n_t + t) * (width // (n_dp * n_t))
-    lines = pltpu.roll(vec[...], lax.rem(width - first, width), 1)
+    first = lax.rem(d * (width // n_dp), BLOCK)
+    lines = pltpu.roll(vec[...], lax.rem(BLOCK - first, BLOCK), 1)
+    shares[6][...] = lines[6:7, : shares[6].shape[1]]
+    first = first + t * (width // (n_dp * n_t))
+    lines = pltpu.roll(vec[...], lax.rem(BLOCK - first, BLOCK), 1)
     for i in range(6):
         shares[i][...] = lines[i : i + 1, : shares[i].shape[1]]
-    lines = pltpu.roll(vec[...], lax.rem(width - d * (hidden_w // n_dp), width), 1)
-    shares[6][...] = lines[6:7, : shares[6].shape[1]]
-    for copy in copies:
-        copy.wait()
+    for _, going in pieces:
+        going.wait()
 
 
 def fused_device(
@@ -976,13 +1073,17 @@
             pltpu.VMEM((n_t, n_h, n_l, n_x, part, w), BF),
             pltpu.VMEM((n_y, n_h, n_l, n_x, part, w), BF),
         ]
-        for axis in ORDER[tag]:
-            if axis == "y":
+        for step in ORDER[tag]:
+            if step == "g":
+                bufs.append(pltpu.VMEM((n_y, n_h, part, w), BF))
+                break
+            if step == "y":
                 early = False
                 lead = (n_y - 1,)
             else:
-                dims = [a for a in dims if a != axis]
-                lead = ((n_y,) if early else ()) + (sizes[axis] - 1,)
+                group = AXES[step]
+                dims = [a for a in dims if a not in group]
+                lead = ((n_y,) if early else ()) + (math.prod(sizes[a] for a in group) - 1,)
             bufs.append(pltpu.VMEM(lead + tuple(sizes[a] for a in dims) + (part, w), BF))
         return bufs
 
@@ -1013,8 +1114,8 @@
         single(rows, width),
         half(rows, width),
         single(rows, width),
-        single(rows, width),
-        half(rows, hidden_w),
+        half(rows, n_t * hidden_w),
+        half(CORES, rows, hidden_w),
         half(rows, hidden_w),
         half(rows, width),
         half(rows, n_t * heads_w),
@@ -1024,12 +1125,11 @@
         single(n_t, 8, width),
         single(n_t - 1, 8, width),
         single(8, width),
-        single(n_dp - 1, 8, width),
+        single(n_dp - 1, 8, BLOCK),
         chunk("u", hidden_w),
         chunk("d", hidden_w),
-        chunk("p", heads_w),
         chunk("qk", 2 * heads_w),
-        chunk("v", heads_w),
+        chunk("pv", 2 * heads_w),
         half(rows, width),
         half(rows, width),
         pltpu.SemaphoreType.DMA((8,)),
@@ -1047,7 +1147,7 @@
             jax.ShapeDtypeStruct((part, heads_w), F32),
             jax.ShapeDtypeStruct((part, hidden_w), F32),
             jax.ShapeDtypeStruct((part, hidden_w), F32),
-            jax.ShapeDtypeStruct((8, width), F32),
+            jax.ShapeDtypeStruct((8, BLOCK), F32),
         ),
         in_specs=[anywhere] * 2 + [near] * 8 + [anywhere] * 4,
         out_specs=[anywhere] * 2 + [near] * 5,
@@ -1073,13 +1173,15 @@
     )
     share = width // (n_dp * n_t)
     out, gtok, gq, gp, gu, gd, *vectors, g_up_bias = pl.pallas_call(
-        functools.partial(result_kernel, (n_t, n_dp, hidden_w)),
+        functools.partial(result_kernel, (n_t, n_dp, width)),
         out_shape=[jax.ShapeDtypeStruct(r.shape, r.dtype) for r in results[:6]]
         + [jax.ShapeDtypeStruct((1, share), F32)] * 6
         + [jax.ShapeDtypeStruct((1, hidden_w // n_dp), F32)],
-        in_specs=[near] * 7,
+        in_specs=[anywhere] * 6 + [near],
         out_specs=[anywhere] * 6 + [near] * 7,
-        scratch_shapes=[pltpu.SemaphoreType.DMA((6,))],
+        scratch_shapes=[pltpu.VMEM(r.shape, r.dtype) for r in results[:6]]
+        + [pltpu.SemaphoreType.DMA((6 * PARTS,))] * 2,
+        compiler_params=pltpu.CompilerParams(vmem_limit_bytes=63 << 20),
     )(*results)
     vectors = [v.reshape(share) for v in vectors]
     return (

time: 86.3 us -> 76 us (0.88)
  Pallas kernels: 85.2 us -> 74.9 us
    pallas_call x1, Pallas kernels: 81.6 us -> 70.9 us  [fused_device(): pl.pallas_call(functools.partial(layer_kernel, (n_t, n_dp, rows, width, h...]
where the time goes in v3:
time: 76 us; the launch traced here: 75.7 us
  Pallas kernels  74.9 us (99%)
  between operations  0.84 us (1%)
    pallas_call x1, Pallas kernels, fused_device(): pl.pallas_call(functools.partial(layer_kernel, (n_t, n_dp, rows, width, h...  70.9 us
    pallas_call x1, Pallas kernels, fused_device(): pl.pallas_call(functools.partial(result_kernel, (n_t, n_dp, width)), out_...  4.01 us

profile of v3, /device:TPU:0, one launch (start us, length us, event | category | flops | bytes accessed | tf_op | source)
XLA Modules:
  0.0 75.7 jit_solution(16727129175509952136)
XLA Ops:
  0.7 70.9 %shard_map.237 = (bf16[1024,512]{1,0:T(8,128)(2,1)}, bf16[1024,512]{1,0:T(8,128)(2,1)}, f32[3,64,128]{2,1,0:T(8,128)}, f32[64,128]{1,0:T(8,128)}, f32[64,512]{1,...) custom-call(bf16[1024,512]{1,0:T(8,128)(2,1)} %bitcast.21, bf16[1024,512]{1,0:T(8,128)(2,1)} %bitcast.22, ...), custom_call_target="tpu_custom_call" | custom-call | tf_op jit(solution)/shard_map/pallas_call | solution.py:1141
  71.5 4.0 %shard_map.238 = (bf16[1024,512]{1,0:T(8,128)(2,1)}, bf16[1024,512]{1,0:T(8,128)(2,1)}, f32[3,64,128]{2,1,0:T(8,128)}, f32[64,128]{1,0:T(8,128)}, f32[64,512]{1,...) custom-call(bf16[1024,512]{1,0:T(8,128)(2,1)} %get-tuple-element.33., ...), custom_call_target="tpu_custom_call" | custom-call | tf_op jit(solution)/shard_map/pallas_call | solution.py:1175

commit v4 on v3

--- a/solution.py
+++ b/solution.py
@@ -280,29 +280,28 @@
 
 ORDER = {"u": "xlg", "d": "lxg", "qk": "xlg", "pv": "ywh"}
 SCHEDULE = {
-    "start": ("wp", "wq", "wu", "wd",),
-    "heads0": ("wp",),
-    "attend0": ("wq",),
+    "start": ("wp", "wq", "wd",),
+    "heads0": ("wu", "wq",),
     "attend1": ("wp", "wq", "wq",),
-    "dact": ("wp", "wu",),
-    "attend2": ("wd",),
-    "hidden": ("wu",),
-    "rows1.1": ("wd",),
-    "mlp1": ("d0",),
-    "rows0.0": ("wu", "u0",),
-    "rows0.1": ("wd",),
+    "dact": ("wp", "wd",),
+    "attend2": ("wp", "wu",),
+    "hidden": ("wd",),
+    "rows1.1": ("wu",),
+    "mlp1": ("d0", "u0",),
+    "rows0.0": ("wd",),
+    "rows0.1": ("wu",),
     "mlp0": ("u0", "d0",),
     "mlp3": ("u1", "d1",),
-    "mlp2": ("d1", "u1", "u0",),
-    "qkv3": ("d0", "qk1", "pv1",),
-    "qkv2": ("qk1", "u1", "pv1",),
-    "qkv1": ("u0", "d0", "qk0", "d1",),
-    "qkv0": ("qk1", "u1", "pv0", "qk0",),
+    "mlp2": ("u1", "u0", "d1",),
+    "qkv3": ("pv1", "qk1", "d0",),
+    "qkv2": ("pv1", "qk1", "u1", "u0",),
+    "qkv1": ("d1", "qk0", "d0", "pv0",),
+    "qkv0": ("qk1", "qk0", "u1",),
     "norm1.0": ("pv0", "pv",),
     "norm1.1": ("vec", "d1",),
-    "out.0": ("qk0", "qk1", "u", "vec", "pv",),
-    "out.1": ("qk0", "vec",),
-    "end": ("d", "pv", "qk",),
+    "out.0": ("qk0", "qk1",),
+    "out.1": ("vec", "pv", "qk0",),
+    "end": ("u", "pv", "vec", "d", "qk",),
 }
 
 
@@ -496,20 +495,6 @@
     def at(i, size, offset=0):
         return pl.ds(pl.multiple_of(i * size + offset, math.gcd(size, offset) if offset else size), size)
 
-    load_tok.wait()
-
-    @pl.loop(0, rows // ROWS)
-    def _(i):
-        here = at(i, ROWS)
-        v = tok[here, :].astype(F32)
-        mean = jnp.mean(v, axis=-1, keepdims=True)
-        centre = v - mean
-        r = lax.rsqrt(jnp.mean(centre * centre, axis=-1, keepdims=True) + epsilon)
-        normed = (centre * r * ln1_gain + ln1_bias).astype(BF)
-        n1[here, :] = normed
-        stats[0, here, :] = jnp.broadcast_to(mean, (ROWS, BLOCK))
-        stats[1, here, :] = jnp.broadcast_to(r, (ROWS, BLOCK))
-
     pl.semaphore_wait(barrier, len(peers))
     copies = Copies(send_sem, recv_sem)
 
@@ -794,6 +779,20 @@
             bu.at[s],
             t_peer((n_y - s // CORES) % n_y, (CORES - s % CORES) % CORES),
         )
+
+    load_tok.wait()
+
+    @pl.loop(0, rows // ROWS)
+    def _(i):
+        here = at(i, ROWS)
+        v = tok[here, :].astype(F32)
+        mean = jnp.mean(v, axis=-1, keepdims=True)
+        centre = v - mean
+        r = lax.rsqrt(jnp.mean(centre * centre, axis=-1, keepdims=True) + epsilon)
+        normed = (centre * r * ln1_gain + ln1_bias).astype(BF)
+        n1[here, :] = normed
+        stats[0, here, :] = jnp.broadcast_to(mean, (ROWS, BLOCK))
+        stats[1, here, :] = jnp.broadcast_to(r, (ROWS, BLOCK))
 
     first_head = lax.broadcasted_iota(jnp.int32, (BLOCK, heads_w), 1) < HD
 

time: 76 us -> 75.6 us (level)
  no operation moved by 1% of the time
where the time goes in v4:
time: 75.6 us; the launch traced here: 75.4 us
  Pallas kernels  74.6 us (99%)
  between operations  0.84 us (1%)
    pallas_call x1, Pallas kernels, fused_device(): pl.pallas_call(functools.partial(layer_kernel, (n_t, n_dp, rows, width, h...  70.5 us
    pallas_call x1, Pallas kernels, fused_device(): pl.pallas_call(functools.partial(result_kernel, (n_t, n_dp, width)), out_...  4.01 us

profile of v4, /device:TPU:0, one launch (start us, length us, event | category | flops | bytes accessed | tf_op | source)
XLA Modules:
  0.0 75.4 jit_solution(1300182232739015087)
XLA Ops:
  0.7 70.5 %shard_map.237 = (bf16[1024,512]{1,0:T(8,128)(2,1)}, bf16[1024,512]{1,0:T(8,128)(2,1)}, f32[3,64,128]{2,1,0:T(8,128)}, f32[64,128]{1,0:T(8,128)}, f32[64,512]{1,...) custom-call(bf16[1024,512]{1,0:T(8,128)(2,1)} %bitcast.21, bf16[1024,512]{1,0:T(8,128)(2,1)} %bitcast.22, ...), custom_call_target="tpu_custom_call" | custom-call | tf_op jit(solution)/shard_map/pallas_call | solution.py:1140
  71.2 4.0 %shard_map.238 = (bf16[1024,512]{1,0:T(8,128)(2,1)}, bf16[1024,512]{1,0:T(8,128)(2,1)}, f32[3,64,128]{2,1,0:T(8,128)}, f32[64,128]{1,0:T(8,128)}, f32[64,512]{1,...) custom-call(bf16[1024,512]{1,0:T(8,128)(2,1)} %get-tuple-element.33., ...), custom_call_target="tpu_custom_call" | custom-call | tf_op jit(solution)/shard_map/pallas_call | solution.py:1174
